TPU v7x, 256 devices: a whole 4x4x8 slice. The times are simulated.
256 devices in a mesh: pair: 64 (over y, z, core), virt: 4 (over x).
Axes of the slice: x: 4, y: 4, z: 8, core: 2. Of those that a mesh axis runs over, the one named last changes fastest.
Arguments:
- amplitudes: bfloat16 [256, 256, 8, 128], P('pair', None, 'virt'), may hold values from -6 to 6
- amp_ids: int32 [256, 16, 8], P('pair', None, 'virt'), may hold values from 0 to 16, as said below
- integrals: bfloat16 [64, 1024, 128], P('virt', 'pair'), may hold values from -0.375 to 0.375
- int_ids: int32 [64, 8], P('virt'), may hold values from 0 to 15, as said below
Outputs:
- symmetrized: bfloat16 [256, 256, 8192], P('pair', None, 'virt')
Inputs may be any that keep to these rules, and one draw needn't show every extreme that they name: `amp_ids`: in each amplitude tile the live slots come first and name distinct tiles; the remaining slots hold 16; a tile has 4 to 8 live slots, both ends reached. `int_ids`: the 8 tiles listed for one column tile are distinct.
All inputs are finite; a program needn't handle non-finite values.
Results may differ from a plain program's by a relative error of at most 0.0052.
Values may be sent and summed in bfloat16 or wider, within the bound.
No kernel may reach another device: no remote copies, remote signals or barrier semaphores. Data moves between devices by JAX's collectives and lax.ppermute only.
A program may use at most 320 MiB of HBM per device.

v0:
```python
import jax
import jax.numpy as jnp
from jax import lax
from jax.sharding import PartitionSpec as P

VB = 128
OJ = 16
NK = 16


def mirror_columns(values):
    tile_width = values.shape[-1] // (2 * (values.shape[-1] // (2 * VB)))
    sub_rows = tile_width // 16
    shape_in = values.shape
    blocks = values.reshape(shape_in[:-1] + (shape_in[-1] // (2 * tile_width), 2, tile_width))
    even_part = blocks[..., 0, :]
    odd_part = blocks[..., 1, :]
    new_even = jnp.swapaxes(odd_part.reshape(odd_part.shape[:-1] + (16, sub_rows)), -1, -2).reshape(
        odd_part.shape
    )
    new_odd = jnp.swapaxes(
        even_part.reshape(even_part.shape[:-1] + (sub_rows, 16)), -1, -2
    ).reshape(even_part.shape)
    return jnp.stack([new_even, new_odd], axis=-2).reshape(shape_in)


def densify(slot_data, slot_ids):
    onehot = (slot_ids[..., None] == jnp.arange(NK, dtype=jnp.int32)).astype(jnp.bfloat16)
    dense_part = jnp.einsum(
        "ijsk,ijsc->ijkc", onehot, slot_data, preferred_element_type=jnp.float32
    )
    return dense_part.astype(jnp.bfloat16).reshape(-1, NK * slot_data.shape[-1])


def contract(dense_amps, gathered, int_ids):
    tile_width = gathered.shape[-1]
    col_tiles = gathered.shape[0]
    onehot = (int_ids[..., None] == jnp.arange(NK, dtype=jnp.int32)).astype(jnp.bfloat16)
    listed = gathered.reshape(col_tiles, int_ids.shape[1], tile_width, tile_width)
    dense_ints = jnp.einsum("bvk,bvrc->krbc", onehot, listed, preferred_element_type=jnp.float32)
    dense_ints = dense_ints.astype(jnp.bfloat16).reshape(NK * tile_width, col_tiles * tile_width)
    return jnp.dot(dense_amps, dense_ints, preferred_element_type=jnp.float32).astype(jnp.bfloat16)


def body(amplitudes, amp_ids, integrals, int_ids):
    first_count, occupied, local_slots, tile_width = amplitudes.shape
    gathered = lax.all_gather(integrals, "pair", axis=1, tiled=True)
    own_data, own_ids = (
        lax.all_gather(amplitudes, "virt", axis=2, tiled=True),
        lax.all_gather(amp_ids.astype(jnp.bfloat16), "virt", axis=2, tiled=True),
    )
    own_rows = jnp.repeat(own_ids.astype(jnp.int32), OJ, axis=1)
    ladder = contract(densify(own_data, own_rows), gathered, int_ids)
    received = lax.all_to_all(
        ladder.reshape(first_count, occupied, -1), "pair", split_axis=1, concat_axis=0, tiled=True
    )
    mirrored = jnp.swapaxes(received, 0, 1)
    total = ladder.reshape(first_count, occupied, -1).astype(jnp.float32) + mirror_columns(
        mirrored
    ).astype(jnp.float32)
    return total.astype(jnp.bfloat16)


def solution(mesh):
    in_specs = (
        P("pair", None, "virt", None),
        P("pair", None, "virt"),
        P("virt", "pair", None),
        P("virt", None),
    )
    out_specs = P("pair", None, "virt")
    return jax.shard_map(body, mesh=mesh, in_specs=in_specs, out_specs=out_specs, check_vma=False)
```

profile of v0, /device:TPU:1, one launch (start us, length us, event | category | flops | bytes accessed | tf_op | source)
XLA Modules:
  0.0 344.7 jit_solution(15823300628509563160)
XLA Ops:
  6.5 1.9 copy.59
  8.4 0.0 all-gather.3.cloned.1.call-update
  8.5 0.0 all-gather.5.cloned.1.call-start
  8.5 0.7 all-gather.5.cloned.1.call-update
  9.2 0.8 copy.61
  10.0 0.7 copy_convert_fusion.1
  10.7 9.2 %all_gather.9 = bf16[4,16,8]{1,0,2:T(4,128)(2,1)S(1)} all-gather(bf16[4,16,2]{1,0,2:T(4,128)(2,1)S(1)} %copy_convert_fusion.1), channel_id=1, replica_groups=mesh['pair'=64,'virt'=4] {'virt'}, dimensions={2}, use_global_device_ids=true | all-gather | bytes 1280 | tf_op jit(solution)/shard_map/all_gather | solution.py:50
  19.9 0.1 copy.58
  20.0 26.4 %all-gather.3.cloned.1.call-done = bf16[4,256,8,128]{3,1,0,2:T(8,128)(2,1)} async-done(((bf16[4,256,2,128]{3,1,0,2:T(8,128)(2,1)}), bf16[4,256,8,128]{3,1,0,2:T(8,128)(2,1)}) %all-gather.3.cloned.1.call-update) | async-done | bytes 2097168 | tf_op jit(solution)/shard_map/all_gather | solution.py:49
  46.4 9.1 %fusion.13 = bf16[4,256,16,128]{3,2,1,0:T(8,128)(2,1)} fusion(bf16[4,256,8,128]{3,1,0,2:T(8,128)(2,1)} %all-gather.3.cloned.1.call-done, s32[4,256,8]{2,1,0:T(8,128)S(1)} %bitcast.55), kind=kOutput, calls=%fused_computation.13 | convolution fusion | flops 35782656 | bytes 6324224 | tf_op jit(solution)/shard_map/ijsk,ijsc->ijkc/dot_general | solution.py:29
  55.5 70.2 %all-gather.5.cloned.1.call-done = bf16[16,1024,128]{2,1,0:T(8,128)(2,1)} async-done(((bf16[16,16,128]{2,1,0:T(8,128)(2,1)}), bf16[16,1024,128]{2,1,0:T(8,128)(2,1)}) %all-gather.5.cloned.1.call-update) | async-done | bytes 4194320 | tf_op jit(solution)/shard_map/all_gather | solution.py:47
  125.8 7.5 %convert_bitcast_fusion = bf16[16,128,16,128]{3,0,1,2:T(8,128)(2,1)} fusion(bf16[16,8,128,128]{3,2,1,0:T(8,128)(2,1)} %bitcast.54, s32[16,8]{1,0:T(8,128)S(1)} %copy.61), kind=kOutput, calls=%fused_computation.5 | convolution fusion | flops 71305216 | bytes 12583424 | tf_op jit(solution)/shard_map/bvk,bvrc->krbc/dot_general | solution.py:40
  133.3 12.2 %copy.63 = bf16[16,128,16,128]{3,2,1,0:T(8,128)(2,1)} copy(bf16[16,128,16,128]{3,0,1,2:T(8,128)(2,1)} %convert_bitcast_fusion) | data formatting | bytes 16777216 | tf_op jit(solution)/shard_map/convert_element_type | solution.py:41
  145.4 11.3 %fusion.8 = bf16[1024,2048]{1,0:T(8,128)(2,1)S(1)} fusion(bf16[256,8,16,128]{3,2,1,0:T(8,128)(2,1)} %bitcast.51, bf16[128,8,16,128]{3,2,1,0:T(8,128)(2,1)S(1)} %bitcast.56), kind=kOutput, calls=%fused_computation.12 | convolution fusion | flops 8592031744 | bytes 16777216 | tf_op jit(solution)/shard_map/dot_general | solution.py:42
  156.7 1.9 copy-done
  158.7 5.2 %copy.65 = bf16[4,256,2048]{2,0,1:T(4,128)(2,1)} copy(bf16[4,256,2048]{2,1,0:T(8,128)(2,1)S(1)} %bitcast.46) | data formatting | bytes 8388608 | tf_op jit(solution)/shard_map/reshape | solution.py:58
  163.9 8.6 %all-to-all-start = ((bf16[4,256,2048]{2,0,1:T(4,128)(2,1)}), bf16[4,256,2048]{2,0,1:T(4,128)(2,1)}, u32[]{:S(2)}, u32[]{:S(2)}) async-start(bf16[4,256,2048]{2,0,1:T(4,128)(2,1)} %copy.65), calls=%async_computation | async-start | bytes 8388608 | tf_op jit(solution)/shard_map/all_to_all | solution.py:54
  172.5 6.3 %copy.64 = bf16[4,256,2048]{1,2,0:T(8,128)(2,1)} copy(bf16[4,256,2048]{2,1,0:T(8,128)(2,1)} %bitcast.47) | data formatting | bytes 8388608 | tf_op jit(solution)/shard_map/reshape | solution.py:58
  178.8 89.6 %all-to-all-done = bf16[4,256,2048]{2,0,1:T(4,128)(2,1)} async-done(((bf16[4,256,2048]{2,0,1:T(4,128)(2,1)}), bf16[4,256,2048]{2,0,1:T(4,128)(2,1)}, u32[]{:S(2)}, u32[]{:S(2)}) %all-to-all-start) | async-done | bytes 4194336 | tf_op jit(solution)/shard_map/all_to_all | solution.py:54
  268.4 12.5 %copy.66 = bf16[64,4,4,2048]{3,2,1,0:T(4,128)(2,1)} copy(bf16[64,4,4,2048]{3,1,2,0:T(4,128)(2,1)} %bitcast.7) | data formatting | bytes 8388608 | tf_op jit(solution)/shard_map/all_to_all | solution.py:54
  280.9 7.7 %reshape.25 = bf16[4,256,8,2,128]{4,3,2,0,1:T(2,128)(2,1)} reshape(bf16[4,256,2048]{2,0,1:T(4,128)(2,1)} %bitcast.48) | data formatting | bytes 8388608 | tf_op jit(solution)/shard_map/reshape | solution.py:15
  288.6 14.4 %fusion.19 = (bf16[4,256,8,1,128]{4,3,2,0,1:T(2,128)(2,1)}, bf16[4,256,8,1,128]{4,3,2,0,1:T(2,128)(2,1)}) fusion(bf16[4,256,8,2,128]{4,3,2,0,1:T(2,128)(2,1)} %reshape.25), kind=kLoop, calls=%fused_computation.22 | loop fusion | bytes 8388608 | tf_op jit(solution)/shard_map/slice | solution.py:17
  302.9 9.2 %copy.74 = bf16[4,256,8,1,128]{1,4,2,0,3:T(8,128)(2,1)S(1)} copy(bf16[4,256,8,1,128]{4,3,2,0,1:T(2,128)(2,1)} %get-tuple-element.5) | data formatting | bytes 4194304
  312.2 2.0 copy.68
  314.1 9.5 %copy.75 = bf16[4,256,8,1,128]{1,4,2,0,3:T(8,128)(2,1)S(1)} copy(bf16[4,256,8,1,128]{4,3,2,0,1:T(2,128)(2,1)} %get-tuple-element.6) | data formatting | bytes 4194304
  323.6 0.9 copy.97
  324.6 0.6 copy-done.2
  325.2 0.5 maximum_convert_fusion
  325.8 1.0 copy.71
  326.8 1.2 copy-done.1
  327.9 3.8 %fusion.3 = bf16[4,256,2048]{1,2,0:T(8,128)(2,1)} fusion(f32[4,256,8,2,128]{1,4,3,2,0:T(8,128)S(1)} %copy.71, bf16[4,256,2048]{1,2,0:T(8,128)(2,1)S(1)} %copy-done.1), kind=kLoop, calls=%fused_computation.4 | loop fusion | flops 6291456 | bytes 16777216 | tf_op jit(solution)/shard_map/convert_element_type | solution.py:61
  331.7 6.2 %copy.72 = bf16[4,256,2048]{2,1,0:T(8,128)(2,1)} copy(bf16[4,256,2048]{1,2,0:T(8,128)(2,1)} %fusion.3) | data formatting | bytes 8388608 | tf_op jit(solution)/shard_map/convert_element_type | solution.py:61
  (8 shorter events, 0.1 us)
Async XLA Ops:
  6.5 39.8 %all-gather.3.cloned.1.call-start = ((), (), s32[]{:S(2)}) async-start(), calls=%async_computation.1 | async-start | bytes 2621440 | tf_op jit(solution)/shard_map/all_gather | solution.py:49
  8.5 117.3 %all-gather.5.cloned.1.call-start = ((), (), s32[]{:S(2)}) async-start(), calls=%async_computation.2 | async-start | bytes 4259840 | tf_op jit(solution)/shard_map/all_gather | solution.py:47
  133.3 12.2 %copy-start.3 = (bf16[4,256,16,128]{3,2,1,0:T(8,128)(2,1)S(1)}, bf16[4,256,16,128]{3,2,1,0:T(8,128)(2,1)}, u32[]{:S(2)}) copy-start(bf16[4,256,16,128]{3,2,1,0:T(8,128)(2,1)} %fusion.13) | copy-start | bytes 12582916
  156.7 2.0 copy-start
  163.9 104.4 %all-to-all-start = ((bf16[4,256,2048]{2,0,1:T(4,128)(2,1)}), bf16[4,256,2048]{2,0,1:T(4,128)(2,1)}, u32[]{:S(2)}, u32[]{:S(2)}) async-start(bf16[4,256,2048]{2,0,1:T(4,128)(2,1)} %copy.65), calls=%async_computation | async-start | bytes 8388608 | tf_op jit(solution)/shard_map/all_to_all | solution.py:54
  323.6 1.6 copy-start.2
  325.8 2.2 copy-start.1
Sparse Core Ops, SparseCore 0:
  9.2 37.1 all-gather.2
  48.9 76.8 all-gather.4
where the time goes:
time: 346 us; the launch traced here: 345 us
  waiting for transfers between devices  187 us (54%)
  local copies, waits for them, and re-layouts  93.6 us (27%)
  matrix products  27.9 us (8%)
  between operations  13.5 us (4%)
  blocking collectives  9.25 us (3%)
  starting transfers between devices  8.61 us (2%)
  other arithmetic  5 us (1%)
    all_to_all x1, waiting for transfers between devices, body(): lax.all_to_all(ladder.reshape(first_count, occupied, -1), 'pair', split_a...  89.6 us
    all_gather x1, waiting for transfers between devices, body(): gathered = lax.all_gather(integrals, 'pair', axis=1, tiled=True)  70.2 us
    all_gather x1, waiting for transfers between devices, body(): lax.all_gather(amplitudes, 'virt', axis=2, tiled=True)  26.4 us
    unnamed x12, local copies, waits for them, and re-layouts  25.1 us
    slice x1, local copies, waits for them, and re-layouts, mirror_columns(): odd_part = blocks[..., 1, :]  14.4 us
    all_to_all x1, local copies, waits for them, and re-layouts, body(): lax.all_to_all(ladder.reshape(first_count, occupied, -1), 'pair', split_a...  12.5 us
    convert_element_type x1, local copies, waits for them, and re-layouts, contract(): dense_ints.astype(jnp.bfloat16)  12.2 us
    reshape x2, local copies, waits for them, and re-layouts, body(): ladder.reshape(first_count, occupied, -1).astype(jnp.float32)  11.5 us
  transfers between devices with their start and end apart: 3, of which 3 were waited for; matrix products, arithmetic and copies ran while one was open for 5% of the time, Pallas kernels for 0%

commit v1 on v0

v1 whole, which is shorter than its diff:
```python
import functools

import jax
import jax.numpy as jnp
import numpy as np
from jax import lax
from jax.experimental import pallas as pl
from jax.experimental.pallas import tpu as pltpu
from jax.sharding import PartitionSpec as P

VB = 128
OJ = 16
NK = 16
NY, NZ, NC, NX = 4, 8, 2, 4
BF = jnp.bfloat16
F32 = jnp.float32


def position(y, z, c):
    return ((y % NY) * NZ + z % NZ) * NC + c % NC


def pair_shift(dy, dz, dc):
    return [
        (position(y, z, c), position(y + dy, z + dz, c + dc))
        for y in range(NY)
        for z in range(NZ)
        for c in range(NC)
    ]


def virt_gather(block):
    shifts = (1, NX - 1, 2)
    return [block] + [
        lax.ppermute(block, "virt", [(x, (x + k) % NX) for x in range(NX)]) for k in shifts
    ]


def mirror_matrices():
    matrix = np.zeros((2, VB, VB), np.float32)
    for a in range(VB // 16):
        for e in range(16):
            matrix[0, a * 16 + e, e * (VB // 16) + a] = 1.0
            matrix[1, e * (VB // 16) + a, a * 16 + e] = 1.0
    return matrix


def own_kernel(amp_ids, int_ids, place, s0, s1, s2, s3, *rest):
    blocks, (mirror, ladder, mirrored, amps, dense, listed) = rest[:8], rest[8:]
    step = pl.program_id(0)
    rows = amps.shape[0]
    shards = (s0, s1, s2, s3)

    @pl.when(step == 0)
    def _():
        def clear(t, carry):
            amps[pl.ds(t * 64, 64), :] = jnp.zeros((64, amps.shape[1]), BF)
            return carry

        lax.fori_loop(0, rows // 64, clear, 0)

        def place_tile(t, carry):
            i, jt = t // 16, t % 16
            row = pl.multiple_of(t * OJ, OJ)
            for n, shard in enumerate(shards):
                for s in range(2):
                    k = amp_ids[n, t * 2 + s]
                    source = pl.multiple_of((i * 2 + s) * 256 + jt * OJ, OJ)
                    amps[pl.ds(row, OJ), pl.ds(pl.multiple_of(k * VB, VB), VB)] = shard[
                        pl.ds(source, OJ), :
                    ]
            return carry

        lax.fori_loop(0, rows // OJ, place_tile, 0)

    dense[...] = jnp.zeros(dense.shape, BF)
    mirrored[...] = jnp.zeros(mirrored.shape, BF)
    for half in range(2):
        b = step * 2 + half
        for n in range(4):
            for core in range(2):
                block = blocks[n * 2 + core]
                c = place[4] if core == 0 else 1 - place[4]
                base = place[n] * 256 + c * OJ
                for z in range(NZ):
                    listed[pl.ds(pl.multiple_of(base + z * 32, OJ), OJ), :] = block[z, half]
        turned = jnp.dot(listed[...], mirror[half], preferred_element_type=F32).astype(BF)
        for v in range(8):
            k = pl.multiple_of(int_ids[b, v] * VB, VB)
            dense[pl.ds(k, VB), pl.ds(half * VB, VB)] = listed[pl.ds(v * VB, VB), :]
            mirrored[pl.ds(k, VB), pl.ds((1 - half) * VB, VB)] = turned[v * VB : (v + 1) * VB]
    for m in range(2):
        part = pl.ds(m * (rows // 2), rows // 2)
        ladder[part, :] = jnp.dot(
            amps[part, : NK * VB], dense[...], preferred_element_type=F32
        ).astype(BF)


def own_ladder(amp_ids, int_ids, place, shards, blocks, mirror):
    rows, pairs = 1024, 8
    shard_spec = pl.BlockSpec((shards[0].shape[0], VB), lambda p: (0, 0))
    block_spec = pl.BlockSpec((NZ, 2, OJ, VB), lambda p: (0, p, 0, 0))
    smem = pl.BlockSpec(memory_space=pltpu.SMEM)
    return pl.pallas_call(
        own_kernel,
        grid=(pairs,),
        in_specs=[smem] * 3
        + [shard_spec] * 4
        + [block_spec] * 8
        + [pl.BlockSpec((2, VB, VB), lambda p: (0, 0, 0))],
        out_specs=[
            pl.BlockSpec((rows, 2 * VB), lambda p: (0, p)),
            pl.BlockSpec((NK * VB, 2 * VB), lambda p: (0, p)),
        ],
        out_shape=[
            jax.ShapeDtypeStruct((rows, pairs * 2 * VB), BF),
            jax.ShapeDtypeStruct((NK * VB, pairs * 2 * VB), BF),
        ],
        scratch_shapes=[
            pltpu.VMEM((rows, (NK + 1) * VB), BF),
            pltpu.VMEM((NK * VB, 2 * VB), BF),
            pltpu.VMEM((8 * VB, VB), BF),
        ],
        compiler_params=pltpu.CompilerParams(vmem_limit_bytes=48 * 2**20),
        cost_estimate=pl.CostEstimate(flops=9 * 10**9, bytes_accessed=24 * 2**20, transcendentals=0),
        name="own_ladder",
    )(amp_ids, int_ids, place, *shards, *blocks, mirror)


def turn_kernel(ids, s0, s1, s2, s3, mirrored, ladder, *rest):
    out, amps = rest[-2:]
    shards = (s0, s1, s2, s3)

    @pl.when(pl.program_id(0) == 0)
    def _():
        def place_rows(t, carry):
            row = pl.multiple_of(t * OJ, OJ)
            slots = [
                jnp.broadcast_to(ids[pl.ds(row, OJ), n : n + 1], (OJ, VB)).astype(BF)
                for n in range(8)
            ]
            for i in range(2):
                values = [
                    shards[n // 2][pl.ds(pl.multiple_of((i * 2 + n % 2) * 256 + row, OJ), OJ), :]
                    for n in range(8)
                ]
                for k in range(NK):
                    total = jnp.zeros((OJ, VB), BF)
                    for n in range(8):
                        total = jnp.where(slots[n] == BF(k), values[n], total)
                    amps[pl.ds(pl.multiple_of(i * 256 + row, OJ), OJ), k * VB : (k + 1) * VB] = total
            return carry

        lax.fori_loop(0, 256 // OJ, place_rows, 0)

    turned = jnp.dot(amps[...], mirrored[...], preferred_element_type=F32).astype(BF)
    out[...] = (ladder[...].astype(F32) + turned.astype(F32)).astype(BF)


def add_turned(half, ids, shards, mirrored, ladder, previous):
    rows, pairs = 512, 8
    shard_spec = pl.BlockSpec((shards[0].shape[0], VB), lambda p: (0, 0))
    operands = [ids, *shards, mirrored, ladder]
    in_specs = (
        [pl.BlockSpec((256, 8), lambda p: (0, 0))]
        + [shard_spec] * 4
        + [
            pl.BlockSpec((NK * VB, 2 * VB), lambda p: (0, p)),
            pl.BlockSpec((rows, 2 * VB), lambda p: (half, p)),
        ]
    )
    aliases = {}
    if previous is not None:
        operands.append(previous)
        in_specs.append(pl.BlockSpec(memory_space=pl.ANY))
        aliases = {len(operands) - 1: 0}
    return pl.pallas_call(
        turn_kernel,
        grid=(pairs,),
        in_specs=in_specs,
        out_specs=pl.BlockSpec((rows, 2 * VB), lambda p: (half, p)),
        out_shape=jax.ShapeDtypeStruct((2 * rows, pairs * 2 * VB), BF),
        scratch_shapes=[pltpu.VMEM((rows, NK * VB), BF)],
        input_output_aliases=aliases,
        compiler_params=pltpu.CompilerParams(vmem_limit_bytes=48 * 2**20),
        cost_estimate=pl.CostEstimate(flops=45 * 10**8, bytes_accessed=16 * 2**20, transcendentals=0),
        name="add_turned",
    )(*operands)


def body(amplitudes, amp_ids, integrals, int_ids):
    z_groups = [[position(y, z, c) for z in range(NZ)] for y in range(NY) for c in range(NC)]
    along_z = lax.all_to_all(
        jnp.broadcast_to(integrals[None], (NZ,) + integrals.shape),
        "pair",
        0,
        0,
        axis_index_groups=z_groups,
    )
    along_y = [along_z] + [lax.ppermute(along_z, "pair", pair_shift(k, 0, 0)) for k in (1, 3, 2)]
    blocks = []
    for block in along_y:
        blocks += [block, lax.ppermute(block, "pair", pair_shift(0, 0, 1))]

    messages = jnp.swapaxes(amplitudes.reshape(4, 64, 8, VB), 0, 1).reshape(64, 32, VB)
    tile_ids = jnp.repeat(jnp.swapaxes(amp_ids, 0, 1).reshape(16, 8), 4, axis=0)
    tile_ids = jnp.pad(tile_ids.astype(BF)[:, None, :], ((0, 0), (0, 7), (0, VB - 8)))
    received = lax.all_to_all(jnp.concatenate([messages, tile_ids], axis=1), "pair", 0, 0)
    turned = jnp.swapaxes(received[:, :32].reshape(256, 8, VB), 0, 1).reshape(2, 1024, VB)
    turned_ids = jnp.transpose(received[:, 32, :8].reshape(256, 2)).reshape(4, VB)
    turned_ids = jnp.pad(turned_ids, ((0, 12), (0, 0)))

    own = jnp.swapaxes(amplitudes, 1, 2).reshape(2048, VB)
    own_ids = jnp.pad(amp_ids.astype(BF).reshape(1, VB), ((0, 15), (0, 0)))
    own_shards = virt_gather(jnp.concatenate([own, own_ids], axis=0))
    own_slots = jnp.concatenate([s[2048:2049] for s in own_shards], axis=0).astype(jnp.int32)

    first_shards = virt_gather(jnp.concatenate([turned[0], turned_ids], axis=0))
    second_shards = virt_gather(turned[1])
    slots = jnp.concatenate([s[1024:1028] for s in first_shards], axis=0).reshape(8, 256)
    slots = jnp.transpose(slots).astype(F32)

    place = lax.axis_index("pair").astype(jnp.int32)
    y, core = place // (NZ * NC), place % NC
    place = jnp.stack([y, (y + 3) % NY, (y + 1) % NY, (y + 2) % NY, core])
    mirror = jnp.asarray(mirror_matrices(), BF)
    ladder, mirrored = own_ladder(own_slots, int_ids, place, own_shards, blocks, mirror)
    out = add_turned(0, slots, first_shards, mirrored, ladder, None)
    out = add_turned(1, slots, second_shards, mirrored, ladder, out)
    return out.reshape(4, 256, 2048)


def solution(mesh):
    in_specs = (
        P("pair", None, "virt", None),
        P("pair", None, "virt"),
        P("virt", "pair", None),
        P("virt", None),
    )
    out_specs = P("pair", None, "virt")
    return jax.shard_map(body, mesh=mesh, in_specs=in_specs, out_specs=out_specs, check_vma=False)
```

time: 346 us -> 136 us (0.39)
  waiting for transfers between devices: 187 us -> 46.8 us
  local copies, waits for them, and re-layouts: 93.6 us -> 6.71 us
  Pallas kernels: 0 us -> 43.4 us
  matrix products: 27.9 us -> 0 us
  starting transfers between devices: 8.61 us -> 36.1 us
  between operations: 13.5 us -> 0.22 us
  blocking collectives: 9.25 us -> 0 us
  other arithmetic: 5 us -> 0.99 us
    all_gather x2 -> x0, waiting for transfers between devices: 96.6 us -> none  [the longest x1 70.2 us: body(): gathered = lax.all_gather(integrals, 'pair', axis=1, tiled=True)]
    all_to_all x1 -> x2, waiting for transfers between devices: 89.6 us -> 28.5 us  [the longest x1 16.8 us: body(): lax.all_to_all(jnp.broadcast_to(integrals[None], (NZ,) + integrals.shape)...]
    pallas_call x0 -> x3, Pallas kernels: none -> 43.4 us  [the longest x2 24.3 us: add_turned(): pl.pallas_call(turn_kernel, grid=(pairs,), in_specs=in_specs, out_specs=p...]
    dot_general x3 -> x0, matrix products: 27.9 us -> none  [the longest x1 11.3 us: contract(): jnp.dot(dense_amps, dense_ints, preferred_element_type=jnp.float32)]
    unnamed x12 -> x11, local copies, waits for them, and re-layouts: 25.1 us -> 2.27 us
    ppermute x0 -> x16, starting transfers between devices: none -> 21.6 us  [the longest x9 13.6 us: virt_gather(): lax.ppermute(block, 'virt', [(x, (x + k) % NX) for x in range(NX)])]
    convert_element_type x4 -> x5, local copies, waits for them, and re-layouts: 19.4 us -> 0.36 us  [the longest x3 0.23 us: body(): tile_ids.astype(BF)[:, None, :]]
    reshape x3 -> x2, local copies, waits for them, and re-layouts: 19.2 us -> 0.16 us  [the longest x1 0.15 us: body(): own_ids = jnp.pad(amp_ids.astype(BF).reshape(1, VB), ((0, 15), (0, 0)))]
  transfers between devices with their start and end apart: 3 -> 18, of which waited for: 3 -> 7; matrix products, arithmetic and copies ran while one was open for 5% -> 3% of each run, Pallas kernels for 0% -> 23%
where the time goes in v1:
time: 136 us; the launch traced here: 134 us
  waiting for transfers between devices  46.8 us (34%)
  Pallas kernels  43.4 us (32%)
  starting transfers between devices  36.1 us (27%)
  local copies, waits for them, and re-layouts  6.71 us (5%)
    pallas_call x2, Pallas kernels, add_turned(): pl.pallas_call(turn_kernel, grid=(pairs,), in_specs=in_specs, out_specs=p...  24.3 us
    pallas_call x1, Pallas kernels, own_ladder(): pl.pallas_call(own_kernel, grid=(pairs,), in_specs=[smem] * 3 + [shard_sp...  19.1 us
    all_to_all x1, waiting for transfers between devices, body(): lax.all_to_all(jnp.broadcast_to(integrals[None], (NZ,) + integrals.shape)...  16.8 us
    ppermute x9, waiting for transfers between devices, virt_gather(): lax.ppermute(block, 'virt', [(x, (x + k) % NX) for x in range(NX)])  15 us
    ppermute x9, starting transfers between devices, virt_gather(): lax.ppermute(block, 'virt', [(x, (x + k) % NX) for x in range(NX)])  13.6 us
    all_to_all x1, waiting for transfers between devices, body(): lax.all_to_all(jnp.concatenate([messages, tile_ids], axis=1), 'pair', 0, 0)  11.7 us
    all_to_all x1, starting transfers between devices, body(): lax.all_to_all(jnp.broadcast_to(integrals[None], (NZ,) + integrals.shape)...  9.01 us
    all_to_all x1, starting transfers between devices, body(): lax.all_to_all(jnp.concatenate([messages, tile_ids], axis=1), 'pair', 0, 0)  5.52 us
  transfers between devices with their start and end apart: 18, of which 7 were waited for; matrix products, arithmetic and copies ran while one was open for 3% of the time, Pallas kernels for 23%

profile of v1, /device:TPU:1, one launch (start us, length us, event | category | flops | bytes accessed | tf_op | source)
XLA Modules:
  0.0 134.3 jit_solution(16440412577487380362)
XLA Ops:
  0.0 1.8 %broadcast_in_dim.5 = bf16[8,16,16,128]{3,2,1,0:T(8,128)(2,1)} broadcast(bf16[16,16,128]{2,1,0:T(8,128)(2,1)} %param.7), dimensions={1,2,3} | broadcast | bytes 589824 | tf_op jit(solution)/shard_map/broadcast_in_dim | solution.py:194
  1.8 9.0 %all-to-all-start.1 = ((bf16[8,16,16,128]{3,2,1,0:T(8,128)(2,1)}), bf16[8,16,16,128]{3,2,1,0:T(8,128)(2,1)S(1)}, u32[]{:S(2)}, u32[]{:S(2)}) async-start(bf16[8,16,16,128]{3,2,1,0:T(8,128)(2,1)} %broadcast_in_dim.5), calls=%async_computation.1 | async-start | bytes 1048576 | tf_op jit(solution)/shard_map/all_to_all | solution.py:193
  11.0 0.9 fusion.2
  12.0 16.8 %all-to-all-done.1.rest_0_ = bf16[8,16,16,128]{3,2,1,0:T(8,128)(2,1)S(1)} async-done(((bf16[8,16,16,128]{3,2,1,0:T(8,128)(2,1)}), bf16[8,16,16,128]{3,2,1,0:T(8,128)(2,1)S(1)}, u32[]{:S(2)}, u32[]{:S(2)}) %all-to-all-start.1) | async-done | bytes 524320 | tf_op jit(solution)/shard_map/all_to_all | solution.py:193
  28.8 5.5 %all-to-all-start = ((bf16[64,40,128]{2,1,0:T(8,128)(2,1)}), bf16[64,40,128]{2,1,0:T(8,128)(2,1)S(1)}, u32[]{:S(2)}, u32[]{:S(2)}) async-start(bf16[64,40,128]{2,1,0:T(8,128)(2,1)} %fusion.2), calls=%async_computation | async-start | bytes 1310720 | tf_op jit(solution)/shard_map/all_to_all | solution.py:208
  34.7 2.8 %collective-permute-start.8 = (bf16[2064,128]{1,0:T(8,128)(2,1)S(1)}, bf16[2064,128]{1,0:T(8,128)(2,1)}, u32[]{:S(2)}, u32[]{:S(2)}) collective-permute-start(bf16[2064,128]{1,0:T(8,128)(2,1)S(1)} %fusion.4.s0), channel_id=1, source_target_pairs={{0,2},{1,3},{2,0},{3,1},{4,6},{5,7},{6,4},{7,5},{8,10},{9,11},{10,... | collective-permute-start | bytes 1585160 | tf_op jit(solution)/shard_map/ppermute | solution.py:35
  37.5 0.9 collective-permute-start.7
  38.4 0.6 collective-permute-start.6
  39.0 3.0 %collective-permute-start.14 = (bf16[8,16,16,128]{3,2,1,0:T(8,128)(2,1)S(1)}, bf16[8,16,16,128]{3,2,1,0:T(8,128)(2,1)}, u32[]{:S(2)}, u32[]{:S(2)}) collective-permute-start(bf16[8,16,16,128]{3,2,1,0:T(8,128)(2,1)S(1)} %all-to-all-done.1.rest_0_), channel_id=1, source_target_pairs={{0,128},{4,132},{8,136},{12,140},{16,144},{20,148},{24,152},{28,15... | collective-permute-start | bytes 1572872 | tf_op jit(solution)/shard_map/ppermute | solution.py:200
  42.0 0.8 collective-permute-start.12
  42.8 11.7 %all-to-all-done = bf16[64,40,128]{2,1,0:T(8,128)(2,1)S(1)} async-done(((bf16[64,40,128]{2,1,0:T(8,128)(2,1)}), bf16[64,40,128]{2,1,0:T(8,128)(2,1)S(1)}, u32[]{:S(2)}, u32[]{:S(2)}) %all-to-all-start) | async-done | bytes 655392 | tf_op jit(solution)/shard_map/all_to_all | solution.py:208
  54.5 0.2 fusion.6
  54.7 1.3 collective-permute-start.10
  56.4 4.6 %collective-permute-done.7.s2 = bf16[2064,128]{1,0:T(8,128)(2,1)S(1)} collective-permute-done((bf16[2064,128]{1,0:T(8,128)(2,1)S(1)}, bf16[2064,128]{1,0:T(8,128)(2,1)S(1)}, u32[]{:S(2)}, u32[]{:S(2)}) %collective-permute-start.7) | collective-permute-done | bytes 528416 | tf_op jit(solution)/shard_map/ppermute | solution.py:35
  60.9 1.7 %collective-permute-start.2 = (bf16[1040,128]{1,0:T(8,128)(2,1)S(1)}, bf16[1040,128]{1,0:T(8,128)(2,1)S(1)}, u32[]{:S(2)}, u32[]{:S(2)}) collective-permute-start(bf16[1040,128]{1,0:T(8,128)(2,1)S(1)} %fusion.5.s0), channel_id=1, source_target_pairs={{0,2},{1,3},{2,0},{3,1},{4,6},{5,7},{6,4},{7,5},{8,10},{9,11},{10,... | collective-permute-start | bytes 798728 | tf_op jit(solution)/shard_map/ppermute | solution.py:35
  62.7 2.5 %collective-permute-start.1 = (bf16[1040,128]{1,0:T(8,128)(2,1)S(1)}, bf16[1040,128]{1,0:T(8,128)(2,1)S(1)}, u32[]{:S(2)}, u32[]{:S(2)}) collective-permute-start(bf16[1040,128]{1,0:T(8,128)(2,1)S(1)} %fusion.5.s0), channel_id=1, source_target_pairs={{0,3},{1,0},{2,1},{3,2},{4,7},{5,4},{6,5},{7,6},{8,11},{9,8},{10,9... | collective-permute-start | bytes 798728 | tf_op jit(solution)/shard_map/ppermute | solution.py:35
  65.2 0.9 collective-permute-start.9
  66.2 3.1 %collective-permute-done.12.rest_4_ = bf16[8,16,16,128]{3,2,1,0:T(8,128)(2,1)} collective-permute-done((bf16[8,16,16,128]{3,2,1,0:T(8,128)(2,1)S(1)}, bf16[8,16,16,128]{3,2,1,0:T(8,128)(2,1)}, u32[]{:S(2)}, u32[]{:S(2)}) %collective-permute-start.12) | collective-permute-done | bytes 524320 | tf_op jit(solution)/shard_map/ppermute | solution.py:200
  69.3 1.4 %collective-permute-start.15 = (bf16[8,16,16,128]{3,2,1,0:T(8,128)(2,1)}, bf16[8,16,16,128]{3,2,1,0:T(8,128)(2,1)}, u32[]{:S(2)}, u32[]{:S(2)}) collective-permute-start(bf16[8,16,16,128]{3,2,1,0:T(8,128)(2,1)} %collective-permute-done.14.rest_6_), channel_id=1, source_target_pairs={{0,4},{4,0},{8,12},{12,8},{16,20},{20,16},{24,28},{28,24},{32,36},... | collective-permute-start | bytes 1572872 | tf_op jit(solution)/shard_map/ppermute | solution.py:203
  70.7 0.3 collective-permute-done.10.rest_2_
  71.0 0.5 collective-permute-start.13
  71.5 5.0 %collective-permute-done.1.s2 = bf16[1040,128]{1,0:T(8,128)(2,1)S(1)} collective-permute-done((bf16[1040,128]{1,0:T(8,128)(2,1)S(1)}, bf16[1040,128]{1,0:T(8,128)(2,1)S(1)}, u32[]{:S(2)}, u32[]{:S(2)}) %collective-permute-start.1) | collective-permute-done | bytes 266272 | tf_op jit(solution)/shard_map/ppermute | solution.py:35
  76.5 1.8 %collective-permute-start = (bf16[1040,128]{1,0:T(8,128)(2,1)S(1)}, bf16[1040,128]{1,0:T(8,128)(2,1)S(1)}, u32[]{:S(2)}, u32[]{:S(2)}) collective-permute-start(bf16[1040,128]{1,0:T(8,128)(2,1)S(1)} %fusion.5.s0), channel_id=1, source_target_pairs={{0,1},{1,2},{2,3},{3,0},{4,5},{5,6},{6,7},{7,4},{8,9},{9,10},{10,1... | collective-permute-start | bytes 798728 | tf_op jit(solution)/shard_map/ppermute | solution.py:35
  78.5 0.6 slice.53
  79.1 0.7 slice.51
  79.9 5.3 %collective-permute-done.s1 = bf16[1040,128]{1,0:T(8,128)(2,1)S(1)} collective-permute-done((bf16[1040,128]{1,0:T(8,128)(2,1)S(1)}, bf16[1040,128]{1,0:T(8,128)(2,1)S(1)}, u32[]{:S(2)}, u32[]{:S(2)}) %collective-permute-start) | collective-permute-done | bytes 266272 | tf_op jit(solution)/shard_map/ppermute | solution.py:35
  85.3 0.8 collective-permute-start.5
  86.2 2.4 %collective-permute-start.4 = (bf16[1024,128]{1,0:T(8,128)(2,1)S(1)}, bf16[1024,128]{1,0:T(8,128)(2,1)S(1)}, u32[]{:S(2)}, u32[]{:S(2)}) collective-permute-start(bf16[1024,128]{1,0:T(8,128)(2,1)S(1)} %bitcast.28), channel_id=1, source_target_pairs={{0,3},{1,0},{2,1},{3,2},{4,7},{5,4},{6,5},{7,6},{8,11},{9,8},{10,9... | collective-permute-start | bytes 786440 | tf_op jit(solution)/shard_map/ppermute | solution.py:35
  88.7 19.1 %own_ladder.1 = (bf16[1024,2048]{1,0:T(8,128)(2,1)}, bf16[2048,2048]{1,0:T(8,128)(2,1)}) custom-call(s32[4,128]{1,0:T(4,128)S(1)} %maximum_convert_fusion.1.amp_ids, s32[16,8]{1,0:T(8,128)S(1)} %copy.29.int_ids, s32[5]{0:T(128)S(1)} %stack.23.place, bf16[2064,128]{1,0:T(8,128)(2,1)S(1)} %fusion.4.s0, bf16[2064,128]{1,0:T(8,128)(2,1)} %collective-permute-done.6.s1, ...), custom_call_target="tpu_custom_call" | custom-call | flops 8999999488 | bytes 25165824 | tf_op jit(solution)/shard_map/own_ladder/pallas_call | solution.py:104
  107.8 2.2 %copy-done = bf16[1024,2048]{1,0:T(8,128)(2,1)S(1)} copy-done((bf16[1024,2048]{1,0:T(8,128)(2,1)S(1)}, bf16[1024,2048]{1,0:T(8,128)(2,1)}, u32[]{:S(2)}) %copy-start) | copy-done | bytes 4194328
  110.0 12.2 %add_turned.2.rest_0_ = bf16[1024,2048]{1,0:T(8,128)(2,1)} custom-call(f32[256,8]{1,0:T(8,128)S(1)} %bitcast.25, bf16[1040,128]{1,0:T(8,128)(2,1)S(1)} %fusion.5.s0, bf16[1040,128]{1,0:T(8,128)(2,1)S(1)} %collective-permute-done.s1, bf16[1040,128]{1,0:T(8,128)(2,1)S(1)} %collective-permute-done.1.s2, bf16[1040,128]{1,0:T(8,128)(2,1)S(1)} %collective-permute-done.2.s3, ...), custom_call_target="tpu_custom_call" | custom-call | flops 4499999744 | bytes 16777216 | tf_op jit(solution)/shard_map/add_turned/pallas_call | solution.py:177
  122.1 12.2 %add_turned.3 = bf16[1024,2048]{1,0:T(8,128)(2,1)} custom-call(f32[256,8]{1,0:T(8,128)S(1)} %bitcast.26, bf16[1024,128]{1,0:T(8,128)(2,1)S(1)} %bitcast.30, bf16[1024,128]{1,0:T(8,128)(2,1)S(1)} %collective-permute-done.3.s1, bf16[1024,128]{1,0:T(8,128)(2,1)S(1)} %collective-permute-done.4.s2, ...), custom_call_target="tpu_custom_call", output_to_operand_aliasing={{}: (7, {})} | custom-call | flops 4499999744 | bytes 16777216 | tf_op jit(solution)/shard_map/add_turned/pallas_call | solution.py:177
  (49 shorter events, 1.4 us)
Async XLA Ops:
  0.0 10.8 %copy-start.4 = (s32[4,16,2]{1,2,0:T(2,128)S(1)}, s32[4,16,2]{1,2,0:T(2,128)}, u32[]{:S(2)}) copy-start(s32[4,16,2]{1,2,0:T(2,128)} %param.6) | copy-start | bytes 1540
  0.0 10.9 %copy-start.2 = (bf16[4,256,2,128]{3,2,1,0:T(2,128)(2,1)S(1)}, bf16[4,256,2,128]{3,2,1,0:T(2,128)(2,1)}, u32[]{:S(2)}) copy-start(bf16[4,256,2,128]{3,2,1,0:T(2,128)(2,1)} %param.5) | copy-start | bytes 1572868
  1.8 27.0 %all-to-all-start.1 = ((bf16[8,16,16,128]{3,2,1,0:T(8,128)(2,1)}), bf16[8,16,16,128]{3,2,1,0:T(8,128)(2,1)S(1)}, u32[]{:S(2)}, u32[]{:S(2)}) async-start(bf16[8,16,16,128]{3,2,1,0:T(8,128)(2,1)} %broadcast_in_dim.5), calls=%async_computation.1 | async-start | bytes 1048576 | tf_op jit(solution)/shard_map/all_to_all | solution.py:193
  28.8 25.7 %all-to-all-start = ((bf16[64,40,128]{2,1,0:T(8,128)(2,1)}), bf16[64,40,128]{2,1,0:T(8,128)(2,1)S(1)}, u32[]{:S(2)}, u32[]{:S(2)}) async-start(bf16[64,40,128]{2,1,0:T(8,128)(2,1)} %fusion.2), calls=%async_computation | async-start | bytes 1310720 | tf_op jit(solution)/shard_map/all_to_all | solution.py:208
  34.7 20.0 %collective-permute-start.8 = (bf16[2064,128]{1,0:T(8,128)(2,1)S(1)}, bf16[2064,128]{1,0:T(8,128)(2,1)}, u32[]{:S(2)}, u32[]{:S(2)}) collective-permute-start(bf16[2064,128]{1,0:T(8,128)(2,1)S(1)} %fusion.4.s0), channel_id=1, source_target_pairs={{0,2},{1,3},{2,0},{3,1},{4,6},{5,7},{6,4},{7,5},{8,10},{9,11},{10,... | collective-permute-start | bytes 1585160 | tf_op jit(solution)/shard_map/ppermute | solution.py:35
  37.5 23.4 %collective-permute-start.7 = (bf16[2064,128]{1,0:T(8,128)(2,1)S(1)}, bf16[2064,128]{1,0:T(8,128)(2,1)S(1)}, u32[]{:S(2)}, u32[]{:S(2)}) collective-permute-start(bf16[2064,128]{1,0:T(8,128)(2,1)S(1)} %fusion.4.s0), channel_id=1, source_target_pairs={{0,3},{1,0},{2,1},{3,2},{4,7},{5,4},{6,5},{7,6},{8,11},{9,8},{10,9... | collective-permute-start | bytes 1585160 | tf_op jit(solution)/shard_map/ppermute | solution.py:35
  38.4 24.3 %collective-permute-start.6 = (bf16[2064,128]{1,0:T(8,128)(2,1)S(1)}, bf16[2064,128]{1,0:T(8,128)(2,1)}, u32[]{:S(2)}, u32[]{:S(2)}) collective-permute-start(bf16[2064,128]{1,0:T(8,128)(2,1)S(1)} %fusion.4.s0), channel_id=1, source_target_pairs={{0,1},{1,2},{2,3},{3,0},{4,5},{5,6},{6,7},{7,4},{8,9},{9,10},{10,1... | collective-permute-start | bytes 1585160 | tf_op jit(solution)/shard_map/ppermute | solution.py:35
  39.0 26.3 %collective-permute-start.14 = (bf16[8,16,16,128]{3,2,1,0:T(8,128)(2,1)S(1)}, bf16[8,16,16,128]{3,2,1,0:T(8,128)(2,1)}, u32[]{:S(2)}, u32[]{:S(2)}) collective-permute-start(bf16[8,16,16,128]{3,2,1,0:T(8,128)(2,1)S(1)} %all-to-all-done.1.rest_0_), channel_id=1, source_target_pairs={{0,128},{4,132},{8,136},{12,140},{16,144},{20,148},{24,152},{28,15... | collective-permute-start | bytes 1572872 | tf_op jit(solution)/shard_map/ppermute | solution.py:200
  42.0 27.3 %collective-permute-start.12 = (bf16[8,16,16,128]{3,2,1,0:T(8,128)(2,1)S(1)}, bf16[8,16,16,128]{3,2,1,0:T(8,128)(2,1)}, u32[]{:S(2)}, u32[]{:S(2)}) collective-permute-start(bf16[8,16,16,128]{3,2,1,0:T(8,128)(2,1)S(1)} %all-to-all-done.1.rest_0_), channel_id=1, source_target_pairs={{0,192},{4,196},{8,200},{12,204},{16,208},{20,212},{24,216},{28,22... | collective-permute-start | bytes 1572872 | tf_op jit(solution)/shard_map/ppermute | solution.py:200
  54.4 23.9 %copy-start.3 = (s32[16,8]{0,1:T(8,128)S(1)}, s32[16,8]{0,1:T(8,128)}, u32[]{:S(2)}) copy-start(s32[16,8]{0,1:T(8,128)} %param.8) | copy-start | bytes 1540
  54.6 34.0 %copy-start.1 = (bf16[2,128,128]{2,1,0:T(8,128)(2,1)S(1)}, bf16[2,128,128]{2,1,0:T(8,128)(2,1)}, u32[]{:S(2)}) copy-start(bf16[2,128,128]{2,1,0:T(8,128)(2,1)} %constant.57.clone.rest_8_) | copy-start | bytes 196612
  54.7 16.3 %collective-permute-start.10 = (bf16[8,16,16,128]{3,2,1,0:T(8,128)(2,1)S(1)}, bf16[8,16,16,128]{3,2,1,0:T(8,128)(2,1)}, u32[]{:S(2)}, u32[]{:S(2)}) collective-permute-start(bf16[8,16,16,128]{3,2,1,0:T(8,128)(2,1)S(1)} %all-to-all-done.1.rest_0_), channel_id=1, source_target_pairs={{0,64},{4,68},{8,72},{12,76},{16,80},{20,84},{24,88},{28,92},{32,9... | collective-permute-start | bytes 1572872 | tf_op jit(solution)/shard_map/ppermute | solution.py:200
  60.9 10.5 %collective-permute-start.2 = (bf16[1040,128]{1,0:T(8,128)(2,1)S(1)}, bf16[1040,128]{1,0:T(8,128)(2,1)S(1)}, u32[]{:S(2)}, u32[]{:S(2)}) collective-permute-start(bf16[1040,128]{1,0:T(8,128)(2,1)S(1)} %fusion.5.s0), channel_id=1, source_target_pairs={{0,2},{1,3},{2,0},{3,1},{4,6},{5,7},{6,4},{7,5},{8,10},{9,11},{10,... | collective-permute-start | bytes 798728 | tf_op jit(solution)/shard_map/ppermute | solution.py:35
  62.7 13.9 %collective-permute-start.1 = (bf16[1040,128]{1,0:T(8,128)(2,1)S(1)}, bf16[1040,128]{1,0:T(8,128)(2,1)S(1)}, u32[]{:S(2)}, u32[]{:S(2)}) collective-permute-start(bf16[1040,128]{1,0:T(8,128)(2,1)S(1)} %fusion.5.s0), channel_id=1, source_target_pairs={{0,3},{1,0},{2,1},{3,2},{4,7},{5,4},{6,5},{7,6},{8,11},{9,8},{10,9... | collective-permute-start | bytes 798728 | tf_op jit(solution)/shard_map/ppermute | solution.py:35
  65.2 21.0 %collective-permute-start.9 = (bf16[8,16,16,128]{3,2,1,0:T(8,128)(2,1)S(1)}, bf16[8,16,16,128]{3,2,1,0:T(8,128)(2,1)}, u32[]{:S(2)}, u32[]{:S(2)}) collective-permute-start(bf16[8,16,16,128]{3,2,1,0:T(8,128)(2,1)S(1)} %all-to-all-done.1.rest_0_), channel_id=1, source_target_pairs={{0,4},{4,0},{8,12},{12,8},{16,20},{20,16},{24,28},{28,24},{32,36},... | collective-permute-start | bytes 1572872 | tf_op jit(solution)/shard_map/ppermute | solution.py:203
  69.3 19.4 %collective-permute-start.15 = (bf16[8,16,16,128]{3,2,1,0:T(8,128)(2,1)}, bf16[8,16,16,128]{3,2,1,0:T(8,128)(2,1)}, u32[]{:S(2)}, u32[]{:S(2)}) collective-permute-start(bf16[8,16,16,128]{3,2,1,0:T(8,128)(2,1)} %collective-permute-done.14.rest_6_), channel_id=1, source_target_pairs={{0,4},{4,0},{8,12},{12,8},{16,20},{20,16},{24,28},{28,24},{32,36},... | collective-permute-start | bytes 1572872 | tf_op jit(solution)/shard_map/ppermute | solution.py:203
  71.0 17.7 %collective-permute-start.13 = (bf16[8,16,16,128]{3,2,1,0:T(8,128)(2,1)}, bf16[8,16,16,128]{3,2,1,0:T(8,128)(2,1)}, u32[]{:S(2)}, u32[]{:S(2)}) collective-permute-start(bf16[8,16,16,128]{3,2,1,0:T(8,128)(2,1)} %collective-permute-done.12.rest_4_), channel_id=1, source_target_pairs={{0,4},{4,0},{8,12},{12,8},{16,20},{20,16},{24,28},{28,24},{32,36},... | collective-permute-start | bytes 1572872 | tf_op jit(solution)/shard_map/ppermute | solution.py:203
  71.5 17.2 %collective-permute-start.11 = (bf16[8,16,16,128]{3,2,1,0:T(8,128)(2,1)}, bf16[8,16,16,128]{3,2,1,0:T(8,128)(2,1)}, u32[]{:S(2)}, u32[]{:S(2)}) collective-permute-start(bf16[8,16,16,128]{3,2,1,0:T(8,128)(2,1)} %collective-permute-done.10.rest_2_), channel_id=1, source_target_pairs={{0,4},{4,0},{8,12},{12,8},{16,20},{20,16},{24,28},{28,24},{32,36},... | collective-permute-start | bytes 1572872 | tf_op jit(solution)/shard_map/ppermute | solution.py:203
  76.5 8.7 %collective-permute-start = (bf16[1040,128]{1,0:T(8,128)(2,1)S(1)}, bf16[1040,128]{1,0:T(8,128)(2,1)S(1)}, u32[]{:S(2)}, u32[]{:S(2)}) collective-permute-start(bf16[1040,128]{1,0:T(8,128)(2,1)S(1)} %fusion.5.s0), channel_id=1, source_target_pairs={{0,1},{1,2},{2,3},{3,0},{4,5},{5,6},{6,7},{7,4},{8,9},{9,10},{10,1... | collective-permute-start | bytes 798728 | tf_op jit(solution)/shard_map/ppermute | solution.py:35
  85.3 36.9 %collective-permute-start.5 = (bf16[1024,128]{1,0:T(8,128)(2,1)S(1)}, bf16[1024,128]{1,0:T(8,128)(2,1)S(1)}, u32[]{:S(2)}, u32[]{:S(2)}) collective-permute-start(bf16[1024,128]{1,0:T(8,128)(2,1)S(1)} %bitcast.27), channel_id=1, source_target_pairs={{0,2},{1,3},{2,0},{3,1},{4,6},{5,7},{6,4},{7,5},{8,10},{9,11},{10,... | collective-permute-start | bytes 786440 | tf_op jit(solution)/shard_map/ppermute | solution.py:35
  86.2 35.9 %collective-permute-start.4 = (bf16[1024,128]{1,0:T(8,128)(2,1)S(1)}, bf16[1024,128]{1,0:T(8,128)(2,1)S(1)}, u32[]{:S(2)}, u32[]{:S(2)}) collective-permute-start(bf16[1024,128]{1,0:T(8,128)(2,1)S(1)} %bitcast.28), channel_id=1, source_target_pairs={{0,3},{1,0},{2,1},{3,2},{4,7},{5,4},{6,5},{7,6},{8,11},{9,8},{10,9... | collective-permute-start | bytes 786440 | tf_op jit(solution)/shard_map/ppermute | solution.py:35
  88.6 33.5 %collective-permute-start.3 = (bf16[1024,128]{1,0:T(8,128)(2,1)S(1)}, bf16[1024,128]{1,0:T(8,128)(2,1)S(1)}, u32[]{:S(2)}, u32[]{:S(2)}) collective-permute-start(bf16[1024,128]{1,0:T(8,128)(2,1)S(1)} %bitcast.29), channel_id=1, source_target_pairs={{0,1},{1,2},{2,3},{3,0},{4,5},{5,6},{6,7},{7,4},{8,9},{9,10},{10,1... | collective-permute-start | bytes 786440 | tf_op jit(solution)/shard_map/ppermute | solution.py:35
  107.8 2.2 %copy-start = (bf16[1024,2048]{1,0:T(8,128)(2,1)S(1)}, bf16[1024,2048]{1,0:T(8,128)(2,1)}, u32[]{:S(2)}) copy-start(bf16[1024,2048]{1,0:T(8,128)(2,1)} %get-tuple-element.8.ladder) | copy-start | bytes 12582916

commit v2 on v0

v2 whole, which is shorter than its diff:
```python
import functools

import jax
import jax.numpy as jnp
import numpy as np
from jax import lax
from jax.experimental import pallas as pl
from jax.experimental.pallas import tpu as pltpu
from jax.sharding import PartitionSpec as P

VB = 128
OJ = 16
NK = 16
NY, NZ, NC, NX = 4, 8, 2, 4
BF = jnp.bfloat16
F32 = jnp.float32


def position(y, z, c):
    return ((y % NY) * NZ + z % NZ) * NC + c % NC


def pair_shift(dy, dz, dc):
    return [
        (position(y, z, c), position(y + dy, z + dz, c + dc))
        for y in range(NY)
        for z in range(NZ)
        for c in range(NC)
    ]


def z_swap():
    return [
        (position(y, z, c), position(y, z ^ 1, c))
        for y in range(NY)
        for z in range(NZ)
        for c in range(NC)
    ]


def virt_shift(block, k):
    return lax.ppermute(block, "virt", [(x, (x + k) % NX) for x in range(NX)])


def mirror_matrix():
    matrix = np.zeros((2 * VB, 2 * VB), np.float32)
    for a in range(VB // 16):
        for e in range(16):
            even, odd = a * 16 + e, VB + e * (VB // 16) + a
            matrix[even, odd] = matrix[odd, even] = 1.0
    return matrix


def spread_rows(int_ids):
    place = lax.axis_index("pair").astype(jnp.int32)
    y, z, core = place // (NZ * NC), place // NC % NZ, place % NC
    at = jnp.arange(4 * NC * NZ, dtype=jnp.int32)
    y = (y + 4 - jnp.asarray([0, 1, 3, 2], jnp.int32)[at // 16]) % NY
    z = (z + 8 - jnp.asarray([0, 2, 6, 4], jnp.int32)[at // 2 % 4]) % NZ
    z = jnp.where(at % 2 == 0, z, z + 1 - 2 * (z % 2))
    core = jnp.where(at // NZ % 2 == 0, core, 1 - core)
    listed = y * 2 + z // 4
    chosen = (listed[:, None] == jnp.arange(8, dtype=jnp.int32)).astype(jnp.int32)
    tiles = jnp.sum(chosen[None] * int_ids[:, None, :], axis=-1)
    return tiles * VB + (z % 4 * 2 + core) * OJ


def params(mib):
    return pltpu.CompilerParams(vmem_limit_bytes=mib * 2**20)


def cost(flops, mib):
    return pl.CostEstimate(flops=flops, bytes_accessed=mib * 2**20, transcendentals=0)


VMEM = pl.BlockSpec(memory_space=pltpu.VMEM)
SMEM = pl.BlockSpec(memory_space=pltpu.SMEM)
ANY = pl.BlockSpec(memory_space=pl.ANY)


def dense_kernel(amp_ids, s0, s1, s2, s3, out, amps):
    shards = (s0, s1, s2, s3)

    def place_tiles(t, carry):
        i, jt = t // 16, t % 16
        amps[...] = jnp.zeros(amps.shape, BF)
        for n, shard in enumerate(shards):
            for s in range(2):
                k = amp_ids[n, t * 2 + s]
                source = pl.multiple_of((i * 2 + s) * 256 + jt * OJ, OJ)
                amps[:, pl.ds(pl.multiple_of(k * VB, VB), VB)] = shard[pl.ds(source, OJ), :]
        out[pl.ds(pl.multiple_of(t * OJ, OJ), OJ), :] = amps[:, : NK * VB]
        return carry

    lax.fori_loop(0, 64, place_tiles, 0)


def dense_own(amp_ids, shards):
    return pl.pallas_call(
        dense_kernel,
        in_specs=[SMEM] + [VMEM] * 4,
        out_specs=VMEM,
        out_shape=jax.ShapeDtypeStruct((1024, NK * VB), BF),
        scratch_shapes=[pltpu.VMEM((OJ, (NK + 1) * VB), BF)],
        compiler_params=params(48),
        cost_estimate=cost(0, 0),
        name="dense_own",
    )(amp_ids, *shards)


def columns(p):
    return pl.ds(pl.multiple_of(p * 2 * VB, 2 * VB), 2 * VB)


def own_kernel(rows, dense_own, *rest):
    blocks, ladder, spread, amps, zeros, dense, sums, sems = rest[:8], *rest[8:]
    fetch = pltpu.make_async_copy(dense_own, amps, sems.at[6])
    fetch.start()
    zeros[...] = jnp.zeros(zeros.shape, BF)

    def store_ladder(p, slot):
        return pltpu.make_async_copy(sums.at[slot], ladder.at[:, columns(p)], sems.at[slot])

    def store_spread(p, slot):
        return pltpu.make_async_copy(dense.at[slot], spread.at[:, columns(p)], sems.at[2 + slot])

    def clear(slot):
        return pltpu.make_async_copy(zeros, dense.at[slot], sems.at[4 + slot])

    clear(0).start()
    clear(1).start()

    def column_pair(p, carry):
        slot = p % 2
        clear(slot).wait()
        for half in range(2):
            b = p * 2 + half
            for n, block in enumerate(blocks):
                for at in range(NZ):
                    row = pl.multiple_of(rows[b, n * NZ + at], OJ)
                    dense[slot, pl.ds(row, OJ), half * VB : (half + 1) * VB] = block[at, b]
        store_spread(p, slot).start()

        @pl.when((p >= 1) & (p < 7))
        def _():
            store_spread(p - 1, 1 - slot).wait()
            clear(1 - slot).start()

        pl.when(p == 0)(fetch.wait)
        pl.when(p >= 2)(lambda: store_ladder(p - 2, slot).wait())
        sums[slot] = jnp.dot(amps[...], dense[slot], preferred_element_type=F32).astype(BF)
        store_ladder(p, slot).start()
        return carry

    lax.fori_loop(0, 8, column_pair, 0)
    for p in (6, 7):
        store_ladder(p, p % 2).wait()
        store_spread(p, p % 2).wait()


def own_ladder(rows, dense, blocks):
    return pl.pallas_call(
        own_kernel,
        in_specs=[SMEM, ANY] + [VMEM] * 8,
        out_specs=[ANY] * 2,
        out_shape=[
            jax.ShapeDtypeStruct((1024, 2048), BF),
            jax.ShapeDtypeStruct((NK * VB, 2048), BF),
        ],
        scratch_shapes=[
            pltpu.VMEM((1024, NK * VB), BF),
            pltpu.VMEM((NK * VB, 2 * VB), BF),
            pltpu.VMEM((2, NK * VB, 2 * VB), BF),
            pltpu.VMEM((2, 1024, 2 * VB), BF),
            pltpu.SemaphoreType.DMA((7,)),
        ],
        compiler_params=params(48),
        cost_estimate=cost(0, 0),
        name="own_ladder",
    )(rows, dense, *blocks)


def turn_kernel(ids, s0, s1, s2, s3, mirror, ladder, spread, out, amps, sums, owns, dense, sems):
    shards = (s0, s1, s2, s3)

    def store(p, slot):
        return pltpu.make_async_copy(sums.at[slot], out.at[:, columns(p)], sems.at[slot])

    def load_ladder(p, slot):
        return pltpu.make_async_copy(ladder.at[:, columns(p)], owns.at[slot], sems.at[2 + slot])

    def load_spread(p, slot):
        return pltpu.make_async_copy(spread.at[:, columns(p)], dense.at[slot], sems.at[4 + slot])

    for p in (0, 1):
        load_ladder(p, p).start()
        load_spread(p, p).start()

    def place_rows(t, carry):
        row = pl.multiple_of(t * OJ, OJ)
        slots = [
            jnp.broadcast_to(ids[pl.ds(row, OJ), n : n + 1], (OJ, VB)).astype(BF) for n in range(8)
        ]
        for i in range(4):
            values = [
                shards[n // 2][pl.ds(pl.multiple_of((i * 2 + n % 2) * 256 + row, OJ), OJ), :]
                for n in range(8)
            ]
            for k in range(NK):
                total = jnp.zeros((OJ, VB), BF)
                for n in range(8):
                    total = jnp.where(slots[n] == BF(k), values[n], total)
                amps[pl.ds(pl.multiple_of(i * 256 + row, OJ), OJ), k * VB : (k + 1) * VB] = total
        return carry

    lax.fori_loop(0, 256 // OJ, place_rows, 0)

    def column_pair(p, carry):
        slot = p % 2
        load_ladder(p, slot).wait()
        load_spread(p, slot).wait()
        pl.when(p >= 2)(lambda: store(p - 2, slot).wait())
        turned = jnp.dot(amps[...], dense[slot], preferred_element_type=F32).astype(BF)
        turned = jnp.dot(turned, mirror[...], preferred_element_type=F32)
        sums[slot] = (owns[slot].astype(F32) + turned).astype(BF)
        store(p, slot).start()

        @pl.when(p < 6)
        def _():
            load_ladder(p + 2, slot).start()
            load_spread(p + 2, slot).start()

        return carry

    lax.fori_loop(0, 8, column_pair, 0)
    store(6, 0).wait()
    store(7, 1).wait()


def add_turned(ids, shards, mirror, ladder, spread):
    return pl.pallas_call(
        turn_kernel,
        in_specs=[VMEM] * 6 + [ANY] * 2,
        out_specs=ANY,
        out_shape=jax.ShapeDtypeStruct((1024, 2048), BF),
        scratch_shapes=[
            pltpu.VMEM((1024, NK * VB), BF),
            pltpu.VMEM((2, 1024, 2 * VB), BF),
            pltpu.VMEM((2, 1024, 2 * VB), BF),
            pltpu.VMEM((2, NK * VB, 2 * VB), BF),
            pltpu.SemaphoreType.DMA((6,)),
        ],
        compiler_params=params(48),
        cost_estimate=cost(0, 0),
        name="add_turned",
    )(ids, *shards, mirror, ladder, spread)


def after(value, *others):
    return lax.optimization_barrier((value, *others))[0]


def body(amplitudes, amp_ids, integrals, int_ids):
    own = jnp.swapaxes(amplitudes, 1, 2).reshape(2048, VB)
    own_ids = jnp.pad(amp_ids.astype(BF).reshape(1, VB), ((0, 15), (0, 0)))
    own = jnp.concatenate([own, own_ids], axis=0)
    own_near = [virt_shift(own, k) for k in (1, 3)]

    swapped = lax.ppermute(integrals, "pair", z_swap())
    couple = jnp.stack([integrals, swapped])
    far = [lax.ppermute(couple, "pair", pair_shift(0, k, 0)) for k in (2, 6, 4)]
    along_z = jnp.concatenate([couple] + far)
    along_y = [along_z] + [lax.ppermute(along_z, "pair", pair_shift(k, 0, 0)) for k in (1, 3, 2)]

    messages = jnp.swapaxes(amplitudes.reshape(4, 64, 8, VB), 0, 1).reshape(64, 32, VB)
    tile_ids = jnp.repeat(jnp.swapaxes(amp_ids, 0, 1).reshape(16, 8), 4, axis=0)
    tile_ids = jnp.pad(tile_ids.astype(BF)[:, None, :], ((0, 0), (0, 7), (0, VB - 8)))
    messages = after(jnp.concatenate([messages, tile_ids], axis=1), *far)
    received = lax.all_to_all(messages, "pair", 0, 0)

    own_shards = [own, *own_near, virt_shift(own, 2)]
    own_slots = jnp.concatenate([s[2048:2049] for s in own_shards], axis=0).astype(jnp.int32)
    dense = dense_own(own_slots, own_shards)

    received = after(received, dense)
    turned = jnp.swapaxes(received[:, :32].reshape(256, 8, VB), 0, 1).reshape(2048, VB)
    turned_ids = jnp.transpose(received[:, 32, :8].reshape(256, 2)).reshape(4, VB)
    turned_ids = jnp.pad(turned_ids, ((0, 12), (0, 0)))
    turned = jnp.concatenate([turned, turned_ids], axis=0)
    shards = [turned] + [virt_shift(turned, k) for k in (1, 3, 2)]
    slots = jnp.concatenate([s[2048:2052] for s in shards], axis=0).reshape(8, 256)
    slots = jnp.transpose(slots).astype(F32)

    blocks = []
    for block in along_y:
        block = after(block, turned)
        blocks += [block, lax.ppermute(block, "pair", pair_shift(0, 0, 1))]

    ladder, spread = own_ladder(spread_rows(int_ids), dense, blocks)
    out = add_turned(slots, shards, jnp.asarray(mirror_matrix(), BF), ladder, spread)
    return out.reshape(4, 256, 2048)


def solution(mesh):
    in_specs = (
        P("pair", None, "virt", None),
        P("pair", None, "virt"),
        P("virt", "pair", None),
        P("virt", None),
    )
    out_specs = P("pair", None, "virt")
    return jax.shard_map(body, mesh=mesh, in_specs=in_specs, out_specs=out_specs, check_vma=False)
```

time: 346 us -> 112 us (0.32)
  waiting for transfers between devices: 187 us -> 26.3 us
  local copies, waits for them, and re-layouts: 93.6 us -> 2.31 us
  Pallas kernels: 0 us -> 38.5 us
  starting transfers between devices: 8.61 us -> 40.8 us
  matrix products: 27.9 us -> 0 us
  between operations: 13.5 us -> 0.41 us
  blocking collectives: 9.25 us -> 0 us
    all_gather x2 -> x0, waiting for transfers between devices: 96.6 us -> none  [the longest x1 70.2 us: body(): gathered = lax.all_gather(integrals, 'pair', axis=1, tiled=True)]
    all_to_all x1, waiting for transfers between devices: 89.6 us -> 0.01 us  [body(): received = lax.all_to_all(messages, 'pair', 0, 0)]
    pallas_call x0 -> x3, Pallas kernels: none -> 38.5 us  [the longest x1 17.2 us: own_ladder(): pl.pallas_call(own_kernel, in_specs=[SMEM, ANY] + [VMEM] * 8, out_specs=[...]
    ppermute x0 -> x17, starting transfers between devices: none -> 30.7 us  [the longest x3 10.4 us: body(): far = [lax.ppermute(couple, 'pair', pair_shift(0, k, 0)) for k in (2, 6, 4)]]
    dot_general x3 -> x0, matrix products: 27.9 us -> none  [the longest x1 11.3 us: contract(): jnp.dot(dense_amps, dense_ints, preferred_element_type=jnp.float32)]
    ppermute x0 -> x17, waiting for transfers between devices: none -> 26.3 us  [the longest x6 16.8 us: virt_shift(): return lax.ppermute(block, 'virt', [(x, (x + k) % NX) for x in range(NX)])]
    unnamed x12 -> x13, local copies, waits for them, and re-layouts: 25.1 us -> 0.16 us
    convert_element_type x4 -> x5, local copies, waits for them, and re-layouts: 19.4 us -> 0.36 us  [the longest x3 0.23 us: body(): tile_ids.astype(BF)[:, None, :]]
  transfers between devices with their start and end apart: 3 -> 18, of which waited for: 3 -> 7; matrix products, arithmetic and copies ran while one was open for 5% -> 4% of each run, Pallas kernels for 0% -> 20%
where the time goes in v2:
time: 112 us; the launch traced here: 111 us
  starting transfers between devices  40.8 us (36%)
  Pallas kernels  38.5 us (34%)
  waiting for transfers between devices  26.3 us (23%)
  other arithmetic  2.74 us (2%)
  local copies, waits for them, and re-layouts  2.31 us (2%)
    pallas_call x1, Pallas kernels, own_ladder(): pl.pallas_call(own_kernel, in_specs=[SMEM, ANY] + [VMEM] * 8, out_specs=[...  17.2 us
    ppermute x6, waiting for transfers between devices, virt_shift(): return lax.ppermute(block, 'virt', [(x, (x + k) % NX) for x in range(NX)])  16.8 us
    pallas_call x1, Pallas kernels, add_turned(): pl.pallas_call(turn_kernel, in_specs=[VMEM] * 6 + [ANY] * 2, out_specs=AN...  16.6 us
    ppermute x3, starting transfers between devices, body(): far = [lax.ppermute(couple, 'pair', pair_shift(0, k, 0)) for k in (2, 6, 4)]  10.4 us
    all_to_all x1, starting transfers between devices, body(): received = lax.all_to_all(messages, 'pair', 0, 0)  10.1 us
    ppermute x6, starting transfers between devices, virt_shift(): return lax.ppermute(block, 'virt', [(x, (x + k) % NX) for x in range(NX)])  8.65 us
    ppermute x3, starting transfers between devices, body(): lax.ppermute(along_z, 'pair', pair_shift(k, 0, 0))  6.07 us
    ppermute x3, waiting for transfers between devices, body(): far = [lax.ppermute(couple, 'pair', pair_shift(0, k, 0)) for k in (2, 6, 4)]  5.53 us
  transfers between devices with their start and end apart: 18, of which 7 were waited for; matrix products, arithmetic and copies ran while one was open for 4% of the time, Pallas kernels for 20%

profile of v2, /device:TPU:1, one launch (start us, length us, event | category | flops | bytes accessed | tf_op | source)
XLA Modules:
  0.0 111.0 jit_solution(9055281088959240540)
XLA Ops:
  0.0 2.5 %collective-permute-start = (bf16[16,16,128]{2,1,0:T(8,128)(2,1)}, bf16[16,16,128]{2,1,0:T(8,128)(2,1)S(1)}, u32[]{:S(2)}, u32[]{:S(2)}) collective-permute-start(bf16[16,16,128]{2,1,0:T(8,128)(2,1)} %param.9), channel_id=1, source_target_pairs={{0,8},{4,12},{8,0},{12,4},{16,24},{20,28},{24,16},{28,20},{32,40},... | collective-permute-start | bytes 196616 | tf_op jit(solution)/shard_map/ppermute | solution.py:269
  2.5 1.9 %collective-permute-done = bf16[16,16,128]{2,1,0:T(8,128)(2,1)S(1)} collective-permute-done((bf16[16,16,128]{2,1,0:T(8,128)(2,1)}, bf16[16,16,128]{2,1,0:T(8,128)(2,1)S(1)}, u32[]{:S(2)}, u32[]{:S(2)}) %collective-permute-start) | collective-permute-done | bytes 65568 | tf_op jit(solution)/shard_map/ppermute | solution.py:269
  4.3 0.9 pad_maximum_fusion
  5.2 3.1 %collective-permute-start.1 = (bf16[2,16,16,128]{3,2,1,0:T(8,128)(2,1)S(1)}, bf16[2,16,16,128]{3,2,1,0:T(8,128)(2,1)S(1)}, u32[]{:S(2)}, u32[]{:S(2)}) collective-permute-start(bf16[2,16,16,128]{3,2,1,0:T(8,128)(2,1)S(1)} %pad_maximum_fusion), channel_id=1, source_target_pairs={{0,16},{4,20},{8,24},{12,28},{16,32},{20,36},{24,40},{28,44},{32,4... | collective-permute-start | bytes 393224 | tf_op jit(solution)/shard_map/ppermute | solution.py:271
  8.3 2.9 %collective-permute-start.2 = (bf16[2,16,16,128]{3,2,1,0:T(8,128)(2,1)S(1)}, bf16[2,16,16,128]{3,2,1,0:T(8,128)(2,1)S(1)}, u32[]{:S(2)}, u32[]{:S(2)}) collective-permute-start(bf16[2,16,16,128]{3,2,1,0:T(8,128)(2,1)S(1)} %pad_maximum_fusion), channel_id=1, source_target_pairs={{0,48},{4,52},{8,56},{12,60},{16,0},{20,4},{24,8},{28,12},{32,16},... | collective-permute-start | bytes 393224 | tf_op jit(solution)/shard_map/ppermute | solution.py:271
  11.2 4.4 %collective-permute-start.3 = (bf16[2,16,16,128]{3,2,1,0:T(8,128)(2,1)S(1)}, bf16[2,16,16,128]{3,2,1,0:T(8,128)(2,1)S(1)}, u32[]{:S(2)}, u32[]{:S(2)}) collective-permute-start(bf16[2,16,16,128]{3,2,1,0:T(8,128)(2,1)S(1)} %pad_maximum_fusion), channel_id=1, source_target_pairs={{0,32},{4,36},{8,40},{12,44},{16,48},{20,52},{24,56},{28,60},{32,0... | collective-permute-start | bytes 393224 | tf_op jit(solution)/shard_map/ppermute | solution.py:271
  15.6 0.7 convert_element_type.44
  16.4 1.1 %copy.40 = bf16[64,4,8,128]{3,2,1,0:T(8,128)(2,1)S(1)} copy(bf16[64,4,8,128]{3,2,0,1:T(8,128)(2,1)} %bitcast.48) | data formatting | bytes 1048576 | tf_op jit(solution)/shard_map/transpose | solution.py:275
  17.5 0.9 fusion.3
  18.5 5.5 %collective-permute-done.3 = bf16[2,16,16,128]{3,2,1,0:T(8,128)(2,1)S(1)} collective-permute-done((bf16[2,16,16,128]{3,2,1,0:T(8,128)(2,1)S(1)}, bf16[2,16,16,128]{3,2,1,0:T(8,128)(2,1)S(1)}, u32[]{:S(2)}, u32[]{:S(2)}) %collective-permute-start.3) | collective-permute-done | bytes 131104 | tf_op jit(solution)/shard_map/ppermute | solution.py:271
  24.0 10.1 %all-to-all-start = ((bf16[64,40,128]{2,1,0:T(8,128)(2,1)}), bf16[64,40,128]{2,1,0:T(8,128)(2,1)S(1)}, u32[]{:S(2)}, u32[]{:S(2)}) async-start(bf16[64,40,128]{2,1,0:T(8,128)(2,1)} %fusion.3), calls=%async_computation | async-start | bytes 1310720 | tf_op jit(solution)/shard_map/all_to_all | solution.py:279
  34.2 0.1 reshape.321
  34.5 1.3 %collective-permute-start.4 = (bf16[2064,128]{1,0:T(8,128)(2,1)S(1)}, bf16[2064,128]{1,0:T(8,128)(2,1)S(1)}, u32[]{:S(2)}, u32[]{:S(2)}) collective-permute-start(bf16[2064,128]{1,0:T(8,128)(2,1)S(1)} %fusion.4.s0), channel_id=1, source_target_pairs={{0,1},{1,2},{2,3},{3,0},{4,5},{5,6},{6,7},{7,4},{8,9},{9,10},{10,1... | collective-permute-start | bytes 1585160 | tf_op jit(solution)/shard_map/ppermute | solution.py:42
  35.8 1.5 %collective-permute-start.5 = (bf16[2064,128]{1,0:T(8,128)(2,1)S(1)}, bf16[2064,128]{1,0:T(8,128)(2,1)S(1)}, u32[]{:S(2)}, u32[]{:S(2)}) collective-permute-start(bf16[2064,128]{1,0:T(8,128)(2,1)S(1)} %fusion.4.s0), channel_id=1, source_target_pairs={{0,3},{1,0},{2,1},{3,2},{4,7},{5,4},{6,5},{7,6},{8,11},{9,8},{10,9... | collective-permute-start | bytes 1585160 | tf_op jit(solution)/shard_map/ppermute | solution.py:42
  37.2 1.5 %collective-permute-start.6 = (bf16[2064,128]{1,0:T(8,128)(2,1)S(1)}, bf16[2064,128]{1,0:T(8,128)(2,1)S(1)}, u32[]{:S(2)}, u32[]{:S(2)}) collective-permute-start(bf16[2064,128]{1,0:T(8,128)(2,1)S(1)} %fusion.4.s0), channel_id=1, source_target_pairs={{0,2},{1,3},{2,0},{3,1},{4,6},{5,7},{6,4},{7,5},{8,10},{9,11},{10,... | collective-permute-start | bytes 1585160 | tf_op jit(solution)/shard_map/ppermute | solution.py:42
  38.9 1.5 %collective-permute-start.11 = (bf16[8,16,16,128]{3,2,1,0:T(8,128)(2,1)S(1)}, bf16[8,16,16,128]{3,2,1,0:T(8,128)(2,1)S(1)}, u32[]{:S(2)}, u32[]{:S(2)}) collective-permute-start(bf16[8,16,16,128]{3,2,1,0:T(8,128)(2,1)S(1)} %constant_dynamic-update-slice_fusion.rest_0_), channel_id=1, source_target_pairs={{0,64},{4,68},{8,72},{12,76},{16,80},{20,84},{24,88},{28,92},{32,9... | collective-permute-start | bytes 1572872 | tf_op jit(solution)/shard_map/ppermute | solution.py:273
  40.4 1.5 %collective-permute-start.13 = (bf16[8,16,16,128]{3,2,1,0:T(8,128)(2,1)S(1)}, bf16[8,16,16,128]{3,2,1,0:T(8,128)(2,1)}, u32[]{:S(2)}, u32[]{:S(2)}) collective-permute-start(bf16[8,16,16,128]{3,2,1,0:T(8,128)(2,1)S(1)} %constant_dynamic-update-slice_fusion.rest_0_), channel_id=1, source_target_pairs={{0,192},{4,196},{8,200},{12,204},{16,208},{20,212},{24,216},{28,22... | collective-permute-start | bytes 1572872 | tf_op jit(solution)/shard_map/ppermute | solution.py:273
  41.9 7.0 %collective-permute-done.4.s1 = bf16[2064,128]{1,0:T(8,128)(2,1)S(1)} collective-permute-done((bf16[2064,128]{1,0:T(8,128)(2,1)S(1)}, bf16[2064,128]{1,0:T(8,128)(2,1)S(1)}, u32[]{:S(2)}, u32[]{:S(2)}) %collective-permute-start.4) | collective-permute-done | bytes 528416 | tf_op jit(solution)/shard_map/ppermute | solution.py:42
  48.9 3.1 %collective-permute-start.15 = (bf16[8,16,16,128]{3,2,1,0:T(8,128)(2,1)S(1)}, bf16[8,16,16,128]{3,2,1,0:T(8,128)(2,1)}, u32[]{:S(2)}, u32[]{:S(2)}) collective-permute-start(bf16[8,16,16,128]{3,2,1,0:T(8,128)(2,1)S(1)} %constant_dynamic-update-slice_fusion.rest_0_), channel_id=1, source_target_pairs={{0,128},{4,132},{8,136},{12,140},{16,144},{20,148},{24,152},{28,15... | collective-permute-start | bytes 1572872 | tf_op jit(solution)/shard_map/ppermute | solution.py:273
  52.0 9.3 %collective-permute-done.6.s3 = bf16[2064,128]{1,0:T(8,128)(2,1)S(1)} collective-permute-done((bf16[2064,128]{1,0:T(8,128)(2,1)S(1)}, bf16[2064,128]{1,0:T(8,128)(2,1)S(1)}, u32[]{:S(2)}, u32[]{:S(2)}) %collective-permute-start.6) | collective-permute-done | bytes 528416 | tf_op jit(solution)/shard_map/ppermute | solution.py:42
  61.3 4.7 %dense_own.1 = bf16[1024,2048]{1,0:T(8,128)(2,1)} custom-call(s32[4,128]{1,0:T(4,128)S(1)} %maximum_convert_fusion.1.amp_ids, bf16[2064,128]{1,0:T(8,128)(2,1)S(1)} %fusion.4.s0, bf16[2064,128]{1,0:T(8,128)(2,1)S(1)} %collective-permute-done.4.s1, bf16[2064,128]{1,0:T(8,128)(2,1)S(1)} %collective-permute-done.5.s2, ...), custom_call_target="tpu_custom_call" | custom-call | tf_op jit(solution)/shard_map/dense_own/pallas_call | solution.py:99
  66.6 1.3 %collective-permute-start.12 = (bf16[8,16,16,128]{3,2,1,0:T(8,128)(2,1)S(1)}, bf16[8,16,16,128]{3,2,1,0:T(8,128)(2,1)}, u32[]{:S(2)}, u32[]{:S(2)}) collective-permute-start(bf16[8,16,16,128]{3,2,1,0:T(8,128)(2,1)S(1)} %collective-permute-done.11.rest_2_), channel_id=1, source_target_pairs={{0,4},{4,0},{8,12},{12,8},{16,20},{20,16},{24,28},{28,24},{32,36},... | collective-permute-start | bytes 1572872 | tf_op jit(solution)/shard_map/ppermute | solution.py:297
  68.1 0.9 collective-permute-start.7
  69.1 1.8 %collective-permute-start.8 = (bf16[2064,128]{1,0:T(8,128)(2,1)S(1)}, bf16[2064,128]{1,0:T(8,128)(2,1)S(1)}, u32[]{:S(2)}, u32[]{:S(2)}) collective-permute-start(bf16[2064,128]{1,0:T(8,128)(2,1)S(1)} %fusion.5.s0), channel_id=1, source_target_pairs={{0,3},{1,0},{2,1},{3,2},{4,7},{5,4},{6,5},{7,6},{8,11},{9,8},{10,9... | collective-permute-start | bytes 1585160 | tf_op jit(solution)/shard_map/ppermute | solution.py:42
  70.9 1.6 %collective-permute-start.9 = (bf16[2064,128]{1,0:T(8,128)(2,1)S(1)}, bf16[2064,128]{1,0:T(8,128)(2,1)S(1)}, u32[]{:S(2)}, u32[]{:S(2)}) collective-permute-start(bf16[2064,128]{1,0:T(8,128)(2,1)S(1)} %fusion.5.s0), channel_id=1, source_target_pairs={{0,2},{1,3},{2,0},{3,1},{4,6},{5,7},{6,4},{7,5},{8,10},{9,11},{10,... | collective-permute-start | bytes 1585160 | tf_op jit(solution)/shard_map/ppermute | solution.py:42
  72.5 1.7 %collective-permute-start.16 = (bf16[8,16,16,128]{3,2,1,0:T(8,128)(2,1)}, bf16[8,16,16,128]{3,2,1,0:T(8,128)(2,1)S(1)}, u32[]{:S(2)}, u32[]{:S(2)}) collective-permute-start(bf16[8,16,16,128]{3,2,1,0:T(8,128)(2,1)} %collective-permute-done.15.rest_6_), channel_id=1, source_target_pairs={{0,4},{4,0},{8,12},{12,8},{16,20},{20,16},{24,28},{28,24},{32,36},... | collective-permute-start | bytes 1572872 | tf_op jit(solution)/shard_map/ppermute | solution.py:297
  74.4 1.5 %collective-permute-done.16.rest_7_ = bf16[8,16,16,128]{3,2,1,0:T(8,128)(2,1)S(1)} collective-permute-done((bf16[8,16,16,128]{3,2,1,0:T(8,128)(2,1)}, bf16[8,16,16,128]{3,2,1,0:T(8,128)(2,1)S(1)}, u32[]{:S(2)}, u32[]{:S(2)}) %collective-permute-start.16) | collective-permute-done | bytes 524320 | tf_op jit(solution)/shard_map/ppermute | solution.py:297
  75.9 0.5 collective-permute-done.10.rest_1_
  76.5 17.2 %own_ladder.1 = (bf16[1024,2048]{1,0:T(8,128)(2,1)}, bf16[2048,2048]{1,0:T(8,128)(2,1)}) custom-call(s32[16,64]{1,0:T(8,128)S(1)} %multiply_add_fusion.rows, bf16[1024,2048]{1,0:T(8,128)(2,1)} %dense_own.1, bf16[8,16,16,128]{3,2,1,0:T(8,128)(2,1)S(1)} %constant_dynamic-update-slice_fusion.rest_0_, ...), custom_call_target="tpu_custom_call" | custom-call | tf_op jit(solution)/shard_map/own_ladder/pallas_call | solution.py:162
  93.7 0.4 collective-permute-done.9.s3
  94.2 0.1 copy.37
  94.3 16.6 %add_turned.1 = bf16[1024,2048]{1,0:T(8,128)(2,1)} custom-call(f32[256,8]{1,0:T(8,128)S(1)} %bitcast.45, bf16[2064,128]{1,0:T(8,128)(2,1)S(1)} %fusion.5.s0, bf16[2064,128]{1,0:T(8,128)(2,1)S(1)} %collective-permute-done.7.s1, bf16[2064,128]{1,0:T(8,128)(2,1)S(1)} %collective-permute-done.8.s2, bf16[2064,128]{1,0:T(8,128)(2,1)S(1)} %collective-permute-done.9.s3, ...), custom_call_target="tpu_custom_call" | custom-call | tf_op jit(solution)/shard_map/add_turned/pallas_call | solution.py:241
  (54 shorter events, 1.4 us)
Async XLA Ops:
  0.0 4.3 %collective-permute-start = (bf16[16,16,128]{2,1,0:T(8,128)(2,1)}, bf16[16,16,128]{2,1,0:T(8,128)(2,1)S(1)}, u32[]{:S(2)}, u32[]{:S(2)}) collective-permute-start(bf16[16,16,128]{2,1,0:T(8,128)(2,1)} %param.9), channel_id=1, source_target_pairs={{0,8},{4,12},{8,0},{12,4},{16,24},{20,28},{24,16},{28,20},{32,40},... | collective-permute-start | bytes 196616 | tf_op jit(solution)/shard_map/ppermute | solution.py:269
  5.2 13.3 %collective-permute-start.1 = (bf16[2,16,16,128]{3,2,1,0:T(8,128)(2,1)S(1)}, bf16[2,16,16,128]{3,2,1,0:T(8,128)(2,1)S(1)}, u32[]{:S(2)}, u32[]{:S(2)}) collective-permute-start(bf16[2,16,16,128]{3,2,1,0:T(8,128)(2,1)S(1)} %pad_maximum_fusion), channel_id=1, source_target_pairs={{0,16},{4,20},{8,24},{12,28},{16,32},{20,36},{24,40},{28,44},{32,4... | collective-permute-start | bytes 393224 | tf_op jit(solution)/shard_map/ppermute | solution.py:271
  8.3 10.2 %collective-permute-start.2 = (bf16[2,16,16,128]{3,2,1,0:T(8,128)(2,1)S(1)}, bf16[2,16,16,128]{3,2,1,0:T(8,128)(2,1)S(1)}, u32[]{:S(2)}, u32[]{:S(2)}) collective-permute-start(bf16[2,16,16,128]{3,2,1,0:T(8,128)(2,1)S(1)} %pad_maximum_fusion), channel_id=1, source_target_pairs={{0,48},{4,52},{8,56},{12,60},{16,0},{20,4},{24,8},{28,12},{32,16},... | collective-permute-start | bytes 393224 | tf_op jit(solution)/shard_map/ppermute | solution.py:271
  11.2 12.8 %collective-permute-start.3 = (bf16[2,16,16,128]{3,2,1,0:T(8,128)(2,1)S(1)}, bf16[2,16,16,128]{3,2,1,0:T(8,128)(2,1)S(1)}, u32[]{:S(2)}, u32[]{:S(2)}) collective-permute-start(bf16[2,16,16,128]{3,2,1,0:T(8,128)(2,1)S(1)} %pad_maximum_fusion), channel_id=1, source_target_pairs={{0,32},{4,36},{8,40},{12,44},{16,48},{20,52},{24,56},{28,60},{32,0... | collective-permute-start | bytes 393224 | tf_op jit(solution)/shard_map/ppermute | solution.py:271
  17.5 16.8 %copy-start.1 = (bf16[4,256,2,128]{3,2,1,0:T(2,128)(2,1)S(1)}, bf16[4,256,2,128]{3,2,1,0:T(2,128)(2,1)}, u32[]{:S(2)}) copy-start(bf16[4,256,2,128]{3,2,1,0:T(2,128)(2,1)} %param.7) | copy-start | bytes 1572868
  24.0 42.1 %all-to-all-start = ((bf16[64,40,128]{2,1,0:T(8,128)(2,1)}), bf16[64,40,128]{2,1,0:T(8,128)(2,1)S(1)}, u32[]{:S(2)}, u32[]{:S(2)}) async-start(bf16[64,40,128]{2,1,0:T(8,128)(2,1)} %fusion.3), calls=%async_computation | async-start | bytes 1310720 | tf_op jit(solution)/shard_map/all_to_all | solution.py:279
  34.3 4.4 %copy-start.2 = (bf16[16,16,128]{2,1,0:T(8,128)(2,1)S(1)}, bf16[16,16,128]{2,1,0:T(8,128)(2,1)}, u32[]{:S(2)}) copy-start(bf16[16,16,128]{2,1,0:T(8,128)(2,1)} %param.9) | copy-start | bytes 196612
  34.5 14.4 %collective-permute-start.4 = (bf16[2064,128]{1,0:T(8,128)(2,1)S(1)}, bf16[2064,128]{1,0:T(8,128)(2,1)S(1)}, u32[]{:S(2)}, u32[]{:S(2)}) collective-permute-start(bf16[2064,128]{1,0:T(8,128)(2,1)S(1)} %fusion.4.s0), channel_id=1, source_target_pairs={{0,1},{1,2},{2,3},{3,0},{4,5},{5,6},{6,7},{7,4},{8,9},{9,10},{10,1... | collective-permute-start | bytes 1585160 | tf_op jit(solution)/shard_map/ppermute | solution.py:42
  35.8 16.2 %collective-permute-start.5 = (bf16[2064,128]{1,0:T(8,128)(2,1)S(1)}, bf16[2064,128]{1,0:T(8,128)(2,1)S(1)}, u32[]{:S(2)}, u32[]{:S(2)}) collective-permute-start(bf16[2064,128]{1,0:T(8,128)(2,1)S(1)} %fusion.4.s0), channel_id=1, source_target_pairs={{0,3},{1,0},{2,1},{3,2},{4,7},{5,4},{6,5},{7,6},{8,11},{9,8},{10,9... | collective-permute-start | bytes 1585160 | tf_op jit(solution)/shard_map/ppermute | solution.py:42
  37.2 24.1 %collective-permute-start.6 = (bf16[2064,128]{1,0:T(8,128)(2,1)S(1)}, bf16[2064,128]{1,0:T(8,128)(2,1)S(1)}, u32[]{:S(2)}, u32[]{:S(2)}) collective-permute-start(bf16[2064,128]{1,0:T(8,128)(2,1)S(1)} %fusion.4.s0), channel_id=1, source_target_pairs={{0,2},{1,3},{2,0},{3,1},{4,6},{5,7},{6,4},{7,5},{8,10},{9,11},{10,... | collective-permute-start | bytes 1585160 | tf_op jit(solution)/shard_map/ppermute | solution.py:42
  38.9 27.7 %collective-permute-start.11 = (bf16[8,16,16,128]{3,2,1,0:T(8,128)(2,1)S(1)}, bf16[8,16,16,128]{3,2,1,0:T(8,128)(2,1)S(1)}, u32[]{:S(2)}, u32[]{:S(2)}) collective-permute-start(bf16[8,16,16,128]{3,2,1,0:T(8,128)(2,1)S(1)} %constant_dynamic-update-slice_fusion.rest_0_), channel_id=1, source_target_pairs={{0,64},{4,68},{8,72},{12,76},{16,80},{20,84},{24,88},{28,92},{32,9... | collective-permute-start | bytes 1572872 | tf_op jit(solution)/shard_map/ppermute | solution.py:273
  40.4 27.5 %collective-permute-start.13 = (bf16[8,16,16,128]{3,2,1,0:T(8,128)(2,1)S(1)}, bf16[8,16,16,128]{3,2,1,0:T(8,128)(2,1)}, u32[]{:S(2)}, u32[]{:S(2)}) collective-permute-start(bf16[8,16,16,128]{3,2,1,0:T(8,128)(2,1)S(1)} %constant_dynamic-update-slice_fusion.rest_0_), channel_id=1, source_target_pairs={{0,192},{4,196},{8,200},{12,204},{16,208},{20,212},{24,216},{28,22... | collective-permute-start | bytes 1572872 | tf_op jit(solution)/shard_map/ppermute | solution.py:273
  48.9 22.0 %collective-permute-start.15 = (bf16[8,16,16,128]{3,2,1,0:T(8,128)(2,1)S(1)}, bf16[8,16,16,128]{3,2,1,0:T(8,128)(2,1)}, u32[]{:S(2)}, u32[]{:S(2)}) collective-permute-start(bf16[8,16,16,128]{3,2,1,0:T(8,128)(2,1)S(1)} %constant_dynamic-update-slice_fusion.rest_0_), channel_id=1, source_target_pairs={{0,128},{4,132},{8,136},{12,140},{16,144},{20,148},{24,152},{28,15... | collective-permute-start | bytes 1572872 | tf_op jit(solution)/shard_map/ppermute | solution.py:273
  66.4 1.5 %copy-start.3 = (s32[16,8]{0,1:T(8,128)S(1)}, s32[16,8]{0,1:T(8,128)}, u32[]{:S(2)}) copy-start(s32[16,8]{0,1:T(8,128)} %param.10) | copy-start | bytes 1540
  66.6 5.9 %collective-permute-start.12 = (bf16[8,16,16,128]{3,2,1,0:T(8,128)(2,1)S(1)}, bf16[8,16,16,128]{3,2,1,0:T(8,128)(2,1)}, u32[]{:S(2)}, u32[]{:S(2)}) collective-permute-start(bf16[8,16,16,128]{3,2,1,0:T(8,128)(2,1)S(1)} %collective-permute-done.11.rest_2_), channel_id=1, source_target_pairs={{0,4},{4,0},{8,12},{12,8},{16,20},{20,16},{24,28},{28,24},{32,36},... | collective-permute-start | bytes 1572872 | tf_op jit(solution)/shard_map/ppermute | solution.py:297
  67.9 6.3 %collective-permute-start.14 = (bf16[8,16,16,128]{3,2,1,0:T(8,128)(2,1)}, bf16[8,16,16,128]{3,2,1,0:T(8,128)(2,1)}, u32[]{:S(2)}, u32[]{:S(2)}) collective-permute-start(bf16[8,16,16,128]{3,2,1,0:T(8,128)(2,1)} %collective-permute-done.13.rest_4_), channel_id=1, source_target_pairs={{0,4},{4,0},{8,12},{12,8},{16,20},{20,16},{24,28},{28,24},{32,36},... | collective-permute-start | bytes 1572872 | tf_op jit(solution)/shard_map/ppermute | solution.py:297
  68.1 25.5 %collective-permute-start.7 = (bf16[2064,128]{1,0:T(8,128)(2,1)S(1)}, bf16[2064,128]{1,0:T(8,128)(2,1)S(1)}, u32[]{:S(2)}, u32[]{:S(2)}) collective-permute-start(bf16[2064,128]{1,0:T(8,128)(2,1)S(1)} %fusion.5.s0), channel_id=1, source_target_pairs={{0,1},{1,2},{2,3},{3,0},{4,5},{5,6},{6,7},{7,4},{8,9},{9,10},{10,1... | collective-permute-start | bytes 1585160 | tf_op jit(solution)/shard_map/ppermute | solution.py:42
  69.1 24.6 %collective-permute-start.8 = (bf16[2064,128]{1,0:T(8,128)(2,1)S(1)}, bf16[2064,128]{1,0:T(8,128)(2,1)S(1)}, u32[]{:S(2)}, u32[]{:S(2)}) collective-permute-start(bf16[2064,128]{1,0:T(8,128)(2,1)S(1)} %fusion.5.s0), channel_id=1, source_target_pairs={{0,3},{1,0},{2,1},{3,2},{4,7},{5,4},{6,5},{7,6},{8,11},{9,8},{10,9... | collective-permute-start | bytes 1585160 | tf_op jit(solution)/shard_map/ppermute | solution.py:42
  70.9 23.3 %collective-permute-start.9 = (bf16[2064,128]{1,0:T(8,128)(2,1)S(1)}, bf16[2064,128]{1,0:T(8,128)(2,1)S(1)}, u32[]{:S(2)}, u32[]{:S(2)}) collective-permute-start(bf16[2064,128]{1,0:T(8,128)(2,1)S(1)} %fusion.5.s0), channel_id=1, source_target_pairs={{0,2},{1,3},{2,0},{3,1},{4,6},{5,7},{6,4},{7,5},{8,10},{9,11},{10,... | collective-permute-start | bytes 1585160 | tf_op jit(solution)/shard_map/ppermute | solution.py:42
  72.5 3.4 %collective-permute-start.16 = (bf16[8,16,16,128]{3,2,1,0:T(8,128)(2,1)}, bf16[8,16,16,128]{3,2,1,0:T(8,128)(2,1)S(1)}, u32[]{:S(2)}, u32[]{:S(2)}) collective-permute-start(bf16[8,16,16,128]{3,2,1,0:T(8,128)(2,1)} %collective-permute-done.15.rest_6_), channel_id=1, source_target_pairs={{0,4},{4,0},{8,12},{12,8},{16,20},{20,16},{24,28},{28,24},{32,36},... | collective-permute-start | bytes 1572872 | tf_op jit(solution)/shard_map/ppermute | solution.py:297
  74.2 2.3 %collective-permute-start.10 = (bf16[8,16,16,128]{3,2,1,0:T(8,128)(2,1)S(1)}, bf16[8,16,16,128]{3,2,1,0:T(8,128)(2,1)S(1)}, u32[]{:S(2)}, u32[]{:S(2)}) collective-permute-start(bf16[8,16,16,128]{3,2,1,0:T(8,128)(2,1)S(1)} %constant_dynamic-update-slice_fusion.rest_0_), channel_id=1, source_target_pairs={{0,4},{4,0},{8,12},{12,8},{16,20},{20,16},{24,28},{28,24},{32,36},... | collective-permute-start | bytes 1572872 | tf_op jit(solution)/shard_map/ppermute | solution.py:297
  74.4 19.9 %copy-start = (bf16[256,256]{1,0:T(8,128)(2,1)S(1)}, bf16[256,256]{1,0:T(8,128)(2,1)}, u32[]{:S(2)}) copy-start(bf16[256,256]{1,0:T(8,128)(2,1)} %constant.160.clone.mirror) | copy-start | bytes 393220

commit v3 on v2

v3 whole, which is shorter than its diff:
```python
import functools

import jax
import jax.numpy as jnp
import numpy as np
from jax import lax
from jax.experimental import pallas as pl
from jax.experimental.pallas import tpu as pltpu
from jax.sharding import PartitionSpec as P

VB = 128
OJ = 16
NK = 16
NY, NZ, NC, NX = 4, 8, 2, 4
BF = jnp.bfloat16
F32 = jnp.float32


def position(y, z, c):
    return ((y % NY) * NZ + z % NZ) * NC + c % NC


def pair_shift(dy, dz, dc):
    return [
        (position(y, z, c), position(y + dy, z + dz, c + dc))
        for y in range(NY)
        for z in range(NZ)
        for c in range(NC)
    ]


def virt_shift(block, k):
    return lax.ppermute(block, "virt", [(x, (x + k) % NX) for x in range(NX)])


def mirror_matrix():
    matrix = np.zeros((2 * VB, 2 * VB), np.float32)
    for a in range(VB // 16):
        for e in range(16):
            even, odd = a * 16 + e, VB + e * (VB // 16) + a
            matrix[even, odd] = matrix[odd, even] = 1.0
    return matrix


def spread_rows(int_ids):
    place = lax.axis_index("pair").astype(jnp.int32)
    y, core = place // (NZ * NC), place % NC
    at = jnp.arange(4 * NC * NZ, dtype=jnp.int32)
    y = (y + 4 - jnp.asarray([0, 1, 3, 2], jnp.int32)[at // 16]) % NY
    z = at % NZ
    core = jnp.where(at // NZ % 2 == 0, core, 1 - core)
    listed = y * 2 + z // 4
    chosen = (listed[:, None] == jnp.arange(8, dtype=jnp.int32)).astype(jnp.int32)
    tiles = jnp.sum(chosen[None] * int_ids[:, None, :], axis=-1)
    return tiles * VB + (z % 4 * 2 + core) * OJ


def params(mib):
    return pltpu.CompilerParams(vmem_limit_bytes=mib * 2**20)


def cost(flops, mib):
    return pl.CostEstimate(flops=flops, bytes_accessed=mib * 2**20, transcendentals=0)


VMEM = pl.BlockSpec(memory_space=pltpu.VMEM)
SMEM = pl.BlockSpec(memory_space=pltpu.SMEM)
ANY = pl.BlockSpec(memory_space=pl.ANY)


WIDE = 4 * VB


def columns(p):
    return pl.ds(pl.multiple_of(p * WIDE, WIDE), WIDE)


def own_kernel(rows, amp_ids, *rest):
    shards, blocks = rest[:4], rest[4:12]
    ladder, spread, amps, zeros, dense, sums, sems = rest[12:]
    zeros[...] = jnp.zeros(zeros.shape, BF)

    def store_ladder(p, slot):
        return pltpu.make_async_copy(sums.at[slot], ladder.at[:, columns(p)], sems.at[slot])

    def store_spread(p, slot):
        return pltpu.make_async_copy(dense.at[slot], spread.at[:, columns(p)], sems.at[2 + slot])

    def clear(slot):
        return pltpu.make_async_copy(zeros, dense.at[slot], sems.at[4 + slot])

    clear(0).start()
    clear(1).start()

    def place_tiles(t, carry):
        i, jt = t // 16, t % 16
        here = pl.ds(pl.multiple_of(t * OJ, OJ), OJ)
        amps[here, :] = jnp.zeros((OJ, amps.shape[1]), BF)
        for n, shard in enumerate(shards):
            for s in range(2):
                k = amp_ids[n, t * 2 + s]
                source = pl.multiple_of((i * 2 + s) * 256 + jt * OJ, OJ)
                amps[here, pl.ds(pl.multiple_of(k * VB, VB), VB)] = shard[pl.ds(source, OJ), :]
        return carry

    lax.fori_loop(0, 64, place_tiles, 0)

    def column_group(p, carry):
        slot = p % 2
        clear(slot).wait()
        for quarter in range(4):
            b = p * 4 + quarter
            for n, block in enumerate(blocks):
                for at in range(NZ):
                    row = pl.multiple_of(rows[b, n * NZ + at], OJ)
                    dense[slot, pl.ds(row, OJ), quarter * VB : (quarter + 1) * VB] = block[at, b]
        store_spread(p, slot).start()

        @pl.when((p >= 1) & (p < 3))
        def _():
            store_spread(p - 1, 1 - slot).wait()
            clear(1 - slot).start()

        pl.when(p >= 2)(lambda: store_ladder(p - 2, slot).wait())
        sums[slot] = jnp.dot(amps[:, : NK * VB], dense[slot], preferred_element_type=F32).astype(BF)
        store_ladder(p, slot).start()
        return carry

    lax.fori_loop(0, 4, column_group, 0)
    for p in (2, 3):
        store_ladder(p, p % 2).wait()
        store_spread(p, p % 2).wait()


def own_ladder(rows, amp_ids, shards, blocks):
    return pl.pallas_call(
        own_kernel,
        in_specs=[SMEM] * 2 + [VMEM] * 12,
        out_specs=[ANY] * 2,
        out_shape=[
            jax.ShapeDtypeStruct((1024, 2048), BF),
            jax.ShapeDtypeStruct((NK * VB, 2048), BF),
        ],
        scratch_shapes=[
            pltpu.VMEM((1024, (NK + 1) * VB), BF),
            pltpu.VMEM((NK * VB, WIDE), BF),
            pltpu.VMEM((2, NK * VB, WIDE), BF),
            pltpu.VMEM((2, 1024, WIDE), BF),
            pltpu.SemaphoreType.DMA((6,)),
        ],
        compiler_params=params(48),
        cost_estimate=cost(0, 0),
        name="own_ladder",
    )(rows, amp_ids, *shards, *blocks)


def turn_kernel(ids, s0, s1, s2, s3, mirror, ladder, spread, out, amps, sums, owns, dense, sems):
    shards = (s0, s1, s2, s3)

    def store(p, slot):
        return pltpu.make_async_copy(sums.at[slot], out.at[:, columns(p)], sems.at[slot])

    def load_ladder(p, slot):
        return pltpu.make_async_copy(ladder.at[:, columns(p)], owns.at[slot], sems.at[2 + slot])

    def load_spread(p, slot):
        return pltpu.make_async_copy(spread.at[:, columns(p)], dense.at[slot], sems.at[4 + slot])

    for p in (0, 1):
        load_ladder(p, p).start()
        load_spread(p, p).start()

    def place_rows(t, carry):
        row = pl.multiple_of(t * OJ, OJ)
        slots = [
            jnp.broadcast_to(ids[pl.ds(row, OJ), n : n + 1], (OJ, VB)).astype(BF) for n in range(8)
        ]
        for i in range(4):
            values = [
                shards[n // 2][pl.ds(pl.multiple_of((i * 2 + n % 2) * 256 + row, OJ), OJ), :]
                for n in range(8)
            ]
            for k in range(NK):
                total = jnp.zeros((OJ, VB), BF)
                for n in range(8):
                    total = jnp.where(slots[n] == BF(k), values[n], total)
                amps[pl.ds(pl.multiple_of(i * 256 + row, OJ), OJ), k * VB : (k + 1) * VB] = total
        return carry

    lax.fori_loop(0, 256 // OJ, place_rows, 0)

    def column_group(p, carry):
        slot = p % 2
        load_ladder(p, slot).wait()
        load_spread(p, slot).wait()
        pl.when(p >= 2)(lambda: store(p - 2, slot).wait())
        turned = jnp.dot(amps[...], dense[slot], preferred_element_type=F32).astype(BF)
        for pair in range(2):
            here = slice(pair * 2 * VB, (pair + 1) * 2 * VB)
            other = jnp.dot(turned[:, here], mirror[...], preferred_element_type=F32)
            sums[slot, :, here] = (owns[slot, :, here].astype(F32) + other).astype(BF)
        store(p, slot).start()

        @pl.when(p < 2)
        def _():
            load_ladder(p + 2, slot).start()
            load_spread(p + 2, slot).start()

        return carry

    lax.fori_loop(0, 4, column_group, 0)
    store(2, 0).wait()
    store(3, 1).wait()


def add_turned(ids, shards, mirror, ladder, spread):
    return pl.pallas_call(
        turn_kernel,
        in_specs=[VMEM] * 6 + [ANY] * 2,
        out_specs=ANY,
        out_shape=jax.ShapeDtypeStruct((1024, 2048), BF),
        scratch_shapes=[
            pltpu.VMEM((1024, NK * VB), BF),
            pltpu.VMEM((2, 1024, WIDE), BF),
            pltpu.VMEM((2, 1024, WIDE), BF),
            pltpu.VMEM((2, NK * VB, WIDE), BF),
            pltpu.SemaphoreType.DMA((6,)),
        ],
        compiler_params=params(48),
        cost_estimate=cost(0, 0),
        name="add_turned",
    )(ids, *shards, mirror, ladder, spread)


def after(value, *others):
    return lax.optimization_barrier((value, *others))[0]


def body(amplitudes, amp_ids, integrals, int_ids):
    own = jnp.swapaxes(amplitudes, 1, 2).reshape(2048, VB)
    own_ids = jnp.pad(amp_ids.astype(BF).reshape(1, VB), ((0, 15), (0, 0)))
    own = jnp.concatenate([own, own_ids], axis=0)
    own_near = [virt_shift(own, k) for k in (1, 3)]

    groups = [[position(y, z, c) for z in range(NZ)] for y in range(NY) for c in range(NC)]
    along_z = jnp.broadcast_to(integrals[None], (NZ,) + integrals.shape)
    along_z = lax.all_to_all(along_z, "pair", 0, 0, axis_index_groups=groups)
    beside = lax.ppermute(along_z, "pair", pair_shift(0, 0, 1))
    along_y = [along_z] + [lax.ppermute(along_z, "pair", pair_shift(k, 0, 0)) for k in (1, 3, 2)]

    messages = jnp.swapaxes(amplitudes.reshape(4, 64, 8, VB), 0, 1).reshape(64, 32, VB)
    tile_ids = jnp.repeat(jnp.swapaxes(amp_ids, 0, 1).reshape(16, 8), 4, axis=0)
    tile_ids = jnp.pad(tile_ids.astype(BF)[:, None, :], ((0, 0), (0, 7), (0, VB - 8)))
    messages = after(jnp.concatenate([messages, tile_ids], axis=1), along_z, *own_near)
    received = lax.all_to_all(messages, "pair", 0, 0)

    own_shards = [own, *own_near, virt_shift(after(own, beside), 2)]
    own_slots = jnp.concatenate([s[2048:2049] for s in own_shards], axis=0).astype(jnp.int32)

    turned = jnp.swapaxes(received[:, :32].reshape(256, 8, VB), 0, 1).reshape(2048, VB)
    turned_ids = jnp.transpose(received[:, 32, :8].reshape(256, 2)).reshape(4, VB)
    turned_ids = jnp.pad(turned_ids, ((0, 12), (0, 0)))
    turned = jnp.concatenate([turned, turned_ids], axis=0)
    shards = [turned] + [virt_shift(turned, k) for k in (1, 3, 2)]
    slots = jnp.concatenate([s[2048:2052] for s in shards], axis=0).reshape(8, 256)
    slots = jnp.transpose(slots).astype(F32)

    blocks = [along_z, beside]
    for block in along_y[1:]:
        block = after(block, turned) if block is along_y[2] or block is along_y[3] else block
        blocks += [block, lax.ppermute(block, "pair", pair_shift(0, 0, 1))]

    ladder, spread = own_ladder(spread_rows(int_ids), own_slots, own_shards, blocks)
    out = add_turned(slots, shards, jnp.asarray(mirror_matrix(), BF), ladder, spread)
    return out.reshape(4, 256, 2048)


def solution(mesh):
    in_specs = (
        P("pair", None, "virt", None),
        P("pair", None, "virt"),
        P("virt", "pair", None),
        P("virt", None),
    )
    out_specs = P("pair", None, "virt")
    return jax.shard_map(body, mesh=mesh, in_specs=in_specs, out_specs=out_specs, check_vma=False)
```

time: 112 us -> 111 us (level)
  waiting for transfers between devices: 26.3 us -> 37.3 us
  Pallas kernels: 38.5 us -> 31.6 us
  starting transfers between devices: 40.8 us -> 34.9 us
  other arithmetic: 2.74 us -> 1.14 us
  local copies, waits for them, and re-layouts: 2.31 us -> 3.65 us
    ppermute x3, waiting for transfers between devices: 0.01 us -> 22.3 us  [body(): lax.ppermute(along_z, 'pair', pair_shift(k, 0, 0))]
    ppermute x4 -> x1, starting transfers between devices: 12.9 us -> 0.54 us  [body(): beside = lax.ppermute(along_z, 'pair', pair_shift(0, 0, 1))]
    all_to_all x0 -> x1, starting transfers between devices: none -> 9.01 us  [body(): along_z = lax.all_to_all(along_z, 'pair', 0, 0, axis_index_groups=groups)]
    ppermute x4 -> x1, waiting for transfers between devices: 7.4 us -> 0.01 us  [body(): beside = lax.ppermute(along_z, 'pair', pair_shift(0, 0, 1))]
    ppermute x6, waiting for transfers between devices: 16.8 us -> 9.97 us  [virt_shift(): return lax.ppermute(block, 'virt', [(x, (x + k) % NX) for x in range(NX)])]
    pallas_call x2 -> x1, Pallas kernels: 21.9 us -> 16.8 us  [own_ladder(): pl.pallas_call(own_kernel, in_specs=[SMEM] * 2 + [VMEM] * 12, out_specs=[...]
    all_to_all x0 -> x1, waiting for transfers between devices: none -> 3.68 us  [body(): along_z = lax.all_to_all(along_z, 'pair', 0, 0, axis_index_groups=groups)]
    ppermute x6, starting transfers between devices: 8.65 us -> 10.5 us  [virt_shift(): return lax.ppermute(block, 'virt', [(x, (x + k) % NX) for x in range(NX)])]
  transfers between devices with their start and end apart: 18 -> 15, of which waited for: 7 -> 6; matrix products, arithmetic and copies ran while one was open for 4% -> 3% of each run, Pallas kernels for 20% -> 15%
where the time goes in v3:
time: 111 us; the launch traced here: 109 us
  waiting for transfers between devices  37.3 us (34%)
  starting transfers between devices  34.9 us (31%)
  Pallas kernels  31.6 us (28%)
  local copies, waits for them, and re-layouts  3.65 us (3%)
  other arithmetic  1.14 us (1%)
    ppermute x3, waiting for transfers between devices, body(): lax.ppermute(along_z, 'pair', pair_shift(k, 0, 0))  22.3 us
    pallas_call x1, Pallas kernels, own_ladder(): pl.pallas_call(own_kernel, in_specs=[SMEM] * 2 + [VMEM] * 12, out_specs=[...  16.8 us
    pallas_call x1, Pallas kernels, add_turned(): pl.pallas_call(turn_kernel, in_specs=[VMEM] * 6 + [ANY] * 2, out_specs=AN...  14.8 us
    ppermute x6, starting transfers between devices, virt_shift(): return lax.ppermute(block, 'virt', [(x, (x + k) % NX) for x in range(NX)])  10.5 us
    ppermute x6, waiting for transfers between devices, virt_shift(): return lax.ppermute(block, 'virt', [(x, (x + k) % NX) for x in range(NX)])  9.97 us
    all_to_all x1, starting transfers between devices, body(): along_z = lax.all_to_all(along_z, 'pair', 0, 0, axis_index_groups=groups)  9.01 us
    all_to_all x1, starting transfers between devices, body(): received = lax.all_to_all(messages, 'pair', 0, 0)  8.3 us
    ppermute x3, starting transfers between devices, body(): lax.ppermute(along_z, 'pair', pair_shift(k, 0, 0))  4.44 us
  transfers between devices with their start and end apart: 15, of which 6 were waited for; matrix products, arithmetic and copies ran while one was open for 3% of the time, Pallas kernels for 15%

profile of v3, /device:TPU:1, one launch (start us, length us, event | category | flops | bytes accessed | tf_op | source)
XLA Modules:
  0.0 109.1 jit_solution(10864991424226569649)
XLA Ops:
  0.0 1.8 %broadcast_in_dim.13 = bf16[8,16,16,128]{3,2,1,0:T(8,128)(2,1)} broadcast(bf16[16,16,128]{2,1,0:T(8,128)(2,1)} %param.8), dimensions={1,2,3} | broadcast | bytes 589824 | tf_op jit(solution)/shard_map/broadcast_in_dim | solution.py:246
  1.8 9.0 %all-to-all-start = ((bf16[8,16,16,128]{3,2,1,0:T(8,128)(2,1)}), bf16[8,16,16,128]{3,2,1,0:T(8,128)(2,1)S(1)}, u32[]{:S(2)}, u32[]{:S(2)}) async-start(bf16[8,16,16,128]{3,2,1,0:T(8,128)(2,1)} %broadcast_in_dim.13), calls=%async_computation | async-start | bytes 1048576 | tf_op jit(solution)/shard_map/all_to_all | solution.py:247
  10.8 0.1 copy.33
  10.9 0.1 reshape.196
  11.2 1.3 %collective-permute-start = (bf16[2064,128]{1,0:T(8,128)(2,1)S(1)}, bf16[2064,128]{1,0:T(8,128)(2,1)S(1)}, u32[]{:S(2)}, u32[]{:S(2)}) collective-permute-start(bf16[2064,128]{1,0:T(8,128)(2,1)S(1)} %fusion.4.rest_0_), channel_id=1, source_target_pairs={{0,1},{1,2},{2,3},{3,0},{4,5},{5,6},{6,7},{7,4},{8,9},{9,10},{10,1... | collective-permute-start | bytes 1585160 | tf_op jit(solution)/shard_map/ppermute | solution.py:33
  12.5 1.5 %collective-permute-start.1 = (bf16[2064,128]{1,0:T(8,128)(2,1)S(1)}, bf16[2064,128]{1,0:T(8,128)(2,1)S(1)}, u32[]{:S(2)}, u32[]{:S(2)}) collective-permute-start(bf16[2064,128]{1,0:T(8,128)(2,1)S(1)} %fusion.4.rest_0_), channel_id=1, source_target_pairs={{0,3},{1,0},{2,1},{3,2},{4,7},{5,4},{6,5},{7,6},{8,11},{9,8},{10,9... | collective-permute-start | bytes 1585160 | tf_op jit(solution)/shard_map/ppermute | solution.py:33
  14.1 0.1 copy.39
  14.2 0.9 fusion.3
  15.1 10.0 %collective-permute-done.rest_1_ = bf16[2064,128]{1,0:T(8,128)(2,1)S(1)} collective-permute-done((bf16[2064,128]{1,0:T(8,128)(2,1)S(1)}, bf16[2064,128]{1,0:T(8,128)(2,1)S(1)}, u32[]{:S(2)}, u32[]{:S(2)}) %collective-permute-start) | collective-permute-done | bytes 528416 | tf_op jit(solution)/shard_map/ppermute | solution.py:33
  25.0 3.7 %all-to-all-done.rest_4_ = bf16[8,16,16,128]{3,2,1,0:T(8,128)(2,1)S(1)} async-done(((bf16[8,16,16,128]{3,2,1,0:T(8,128)(2,1)}), bf16[8,16,16,128]{3,2,1,0:T(8,128)(2,1)S(1)}, u32[]{:S(2)}, u32[]{:S(2)}) %all-to-all-start) | async-done | bytes 524320 | tf_op jit(solution)/shard_map/all_to_all | solution.py:247
  28.7 8.3 %all-to-all-start.1 = ((bf16[64,40,128]{2,1,0:T(8,128)(2,1)}), bf16[64,40,128]{2,1,0:T(8,128)(2,1)S(1)}, u32[]{:S(2)}, u32[]{:S(2)}) async-start(bf16[64,40,128]{2,1,0:T(8,128)(2,1)} %fusion.3), calls=%async_computation.1 | async-start | bytes 1310720 | tf_op jit(solution)/shard_map/all_to_all | solution.py:255
  37.0 0.5 collective-permute-start.5
  37.6 1.3 %collective-permute-start.7 = (bf16[8,16,16,128]{3,2,1,0:T(8,128)(2,1)S(1)}, bf16[8,16,16,128]{3,2,1,0:T(8,128)(2,1)}, u32[]{:S(2)}, u32[]{:S(2)}) collective-permute-start(bf16[8,16,16,128]{3,2,1,0:T(8,128)(2,1)S(1)} %all-to-all-done.rest_4_), channel_id=1, source_target_pairs={{0,64},{4,68},{8,72},{12,76},{16,80},{20,84},{24,88},{28,92},{32,9... | collective-permute-start | bytes 1572872 | tf_op jit(solution)/shard_map/ppermute | solution.py:249
  38.9 1.5 %collective-permute-start.9 = (bf16[8,16,16,128]{3,2,1,0:T(8,128)(2,1)S(1)}, bf16[8,16,16,128]{3,2,1,0:T(8,128)(2,1)}, u32[]{:S(2)}, u32[]{:S(2)}) collective-permute-start(bf16[8,16,16,128]{3,2,1,0:T(8,128)(2,1)S(1)} %all-to-all-done.rest_4_), channel_id=1, source_target_pairs={{0,192},{4,196},{8,200},{12,204},{16,208},{20,212},{24,216},{28,22... | collective-permute-start | bytes 1572872 | tf_op jit(solution)/shard_map/ppermute | solution.py:249
  40.4 1.6 %collective-permute-start.11 = (bf16[8,16,16,128]{3,2,1,0:T(8,128)(2,1)S(1)}, bf16[8,16,16,128]{3,2,1,0:T(8,128)(2,1)}, u32[]{:S(2)}, u32[]{:S(2)}) collective-permute-start(bf16[8,16,16,128]{3,2,1,0:T(8,128)(2,1)S(1)} %all-to-all-done.rest_4_), channel_id=1, source_target_pairs={{0,128},{4,132},{8,136},{12,140},{16,144},{20,148},{24,152},{28,15... | collective-permute-start | bytes 1572872 | tf_op jit(solution)/shard_map/ppermute | solution.py:249
  42.1 2.4 %collective-permute-start.6 = (bf16[2064,128]{1,0:T(8,128)(2,1)S(1)}, bf16[2064,128]{1,0:T(8,128)(2,1)}, u32[]{:S(2)}, u32[]{:S(2)}) collective-permute-start(bf16[2064,128]{1,0:T(8,128)(2,1)S(1)} %fusion.4.rest_0_), channel_id=1, source_target_pairs={{0,2},{1,3},{2,0},{3,1},{4,6},{5,7},{6,4},{7,5},{8,10},{9,11},{10,... | collective-permute-start | bytes 1585160 | tf_op jit(solution)/shard_map/ppermute | solution.py:33
  44.5 15.0 %collective-permute-done.7.rest_6_ = bf16[8,16,16,128]{3,2,1,0:T(8,128)(2,1)} collective-permute-done((bf16[8,16,16,128]{3,2,1,0:T(8,128)(2,1)S(1)}, bf16[8,16,16,128]{3,2,1,0:T(8,128)(2,1)}, u32[]{:S(2)}, u32[]{:S(2)}) %collective-permute-start.7) | collective-permute-done | bytes 524320 | tf_op jit(solution)/shard_map/ppermute | solution.py:249
  59.4 0.6 collective-permute-start.8
  60.2 0.1 slice_reduce_fusion
  60.7 1.3 %collective-permute-start.2 = (bf16[2064,128]{1,0:T(8,128)(2,1)S(1)}, bf16[2064,128]{1,0:T(8,128)(2,1)S(1)}, u32[]{:S(2)}, u32[]{:S(2)}) collective-permute-start(bf16[2064,128]{1,0:T(8,128)(2,1)S(1)} %fusion.5.s0), channel_id=1, source_target_pairs={{0,1},{1,2},{2,3},{3,0},{4,5},{5,6},{6,7},{7,4},{8,9},{9,10},{10,1... | collective-permute-start | bytes 1585160 | tf_op jit(solution)/shard_map/ppermute | solution.py:33
  62.0 1.6 %collective-permute-start.3 = (bf16[2064,128]{1,0:T(8,128)(2,1)S(1)}, bf16[2064,128]{1,0:T(8,128)(2,1)S(1)}, u32[]{:S(2)}, u32[]{:S(2)}) collective-permute-start(bf16[2064,128]{1,0:T(8,128)(2,1)S(1)} %fusion.5.s0), channel_id=1, source_target_pairs={{0,3},{1,0},{2,1},{3,2},{4,7},{5,4},{6,5},{7,6},{8,11},{9,8},{10,9... | collective-permute-start | bytes 1585160 | tf_op jit(solution)/shard_map/ppermute | solution.py:33
  63.5 7.3 %collective-permute-done.11.rest_10_ = bf16[8,16,16,128]{3,2,1,0:T(8,128)(2,1)} collective-permute-done((bf16[8,16,16,128]{3,2,1,0:T(8,128)(2,1)S(1)}, bf16[8,16,16,128]{3,2,1,0:T(8,128)(2,1)}, u32[]{:S(2)}, u32[]{:S(2)}) %collective-permute-start.11) | collective-permute-done | bytes 524320 | tf_op jit(solution)/shard_map/ppermute | solution.py:249
  70.9 2.4 %collective-permute-start.4 = (bf16[2064,128]{1,0:T(8,128)(2,1)S(1)}, bf16[2064,128]{1,0:T(8,128)(2,1)S(1)}, u32[]{:S(2)}, u32[]{:S(2)}) collective-permute-start(bf16[2064,128]{1,0:T(8,128)(2,1)S(1)} %fusion.5.s0), channel_id=1, source_target_pairs={{0,2},{1,3},{2,0},{3,1},{4,6},{5,7},{6,4},{7,5},{8,10},{9,11},{10,... | collective-permute-start | bytes 1585160 | tf_op jit(solution)/shard_map/ppermute | solution.py:33
  73.3 1.2 %collective-permute-start.10 = (bf16[8,16,16,128]{3,2,1,0:T(8,128)(2,1)}, bf16[8,16,16,128]{3,2,1,0:T(8,128)(2,1)S(1)}, u32[]{:S(2)}, u32[]{:S(2)}) collective-permute-start(bf16[8,16,16,128]{3,2,1,0:T(8,128)(2,1)} %collective-permute-done.9.rest_8_), channel_id=1, source_target_pairs={{0,4},{4,0},{8,12},{12,8},{16,20},{20,16},{24,28},{28,24},{32,36},... | collective-permute-start | bytes 1572872 | tf_op jit(solution)/shard_map/ppermute | solution.py:271
  74.6 0.3 collective-permute-start.12
  74.8 0.1 multiply_reduce_fusion
  75.0 0.7 slice.46
  75.7 0.6 collective-permute-done.10.rest_9_
  76.3 0.7 collective-permute-done.12.rest_11_
  77.1 16.8 %own_ladder.1 = (bf16[1024,2048]{1,0:T(8,128)(2,1)}, bf16[2048,2048]{1,0:T(8,128)(2,1)}) custom-call(s32[16,64]{1,0:T(8,128)S(1)} %multiply_add_fusion.rows, s32[4,128]{1,0:T(4,128)S(1)} %maximum_convert_fusion.1.amp_ids, bf16[2064,128]{1,0:T(8,128)(2,1)S(1)} %fusion.4.rest_0_, bf16[2064,128]{1,0:T(8,128)(2,1)S(1)} %copy-done.1, ...), custom_call_target="tpu_custom_call" | custom-call | tf_op jit(solution)/shard_map/own_ladder/pallas_call | solution.py:136
  93.9 0.1 copy.36
  94.1 14.8 %add_turned.1 = bf16[1024,2048]{1,0:T(8,128)(2,1)} custom-call(f32[256,8]{1,0:T(8,128)S(1)} %bitcast.25, bf16[2064,128]{1,0:T(8,128)(2,1)S(1)} %fusion.5.s0, bf16[2064,128]{1,0:T(8,128)(2,1)S(1)} %collective-permute-done.2.s1, bf16[2064,128]{1,0:T(8,128)(2,1)S(1)} %collective-permute-done.3.s2, bf16[2064,128]{1,0:T(8,128)(2,1)S(1)} %collective-permute-done.4.s3, ...), custom_call_target="tpu_custom_call" | custom-call | tf_op jit(solution)/shard_map/add_turned/pallas_call | solution.py:217
  (54 shorter events, 0.8 us)
Async XLA Ops:
  0.0 10.8 %copy-start.9 = (s32[4,16,2]{1,2,0:T(2,128)S(1)}, s32[4,16,2]{1,2,0:T(2,128)}, u32[]{:S(2)}) copy-start(s32[4,16,2]{1,2,0:T(2,128)} %param.7) | copy-start | bytes 1540
  0.0 11.1 %copy-start.7 = (bf16[4,256,2,128]{3,2,1,0:T(2,128)(2,1)S(1)}, bf16[4,256,2,128]{3,2,1,0:T(2,128)(2,1)}, u32[]{:S(2)}) copy-start(bf16[4,256,2,128]{3,2,1,0:T(2,128)(2,1)} %param.6) | copy-start | bytes 1572868
  1.8 27.0 %all-to-all-start = ((bf16[8,16,16,128]{3,2,1,0:T(8,128)(2,1)}), bf16[8,16,16,128]{3,2,1,0:T(8,128)(2,1)S(1)}, u32[]{:S(2)}, u32[]{:S(2)}) async-start(bf16[8,16,16,128]{3,2,1,0:T(8,128)(2,1)} %broadcast_in_dim.13), calls=%async_computation | async-start | bytes 1048576 | tf_op jit(solution)/shard_map/all_to_all | solution.py:247
  11.2 13.8 %collective-permute-start = (bf16[2064,128]{1,0:T(8,128)(2,1)S(1)}, bf16[2064,128]{1,0:T(8,128)(2,1)S(1)}, u32[]{:S(2)}, u32[]{:S(2)}) collective-permute-start(bf16[2064,128]{1,0:T(8,128)(2,1)S(1)} %fusion.4.rest_0_), channel_id=1, source_target_pairs={{0,1},{1,2},{2,3},{3,0},{4,5},{5,6},{6,7},{7,4},{8,9},{9,10},{10,1... | collective-permute-start | bytes 1585160 | tf_op jit(solution)/shard_map/ppermute | solution.py:33
  12.5 12.6 %collective-permute-start.1 = (bf16[2064,128]{1,0:T(8,128)(2,1)S(1)}, bf16[2064,128]{1,0:T(8,128)(2,1)S(1)}, u32[]{:S(2)}, u32[]{:S(2)}) collective-permute-start(bf16[2064,128]{1,0:T(8,128)(2,1)S(1)} %fusion.4.rest_0_), channel_id=1, source_target_pairs={{0,3},{1,0},{2,1},{3,2},{4,7},{5,4},{6,5},{7,6},{8,11},{9,8},{10,9... | collective-permute-start | bytes 1585160 | tf_op jit(solution)/shard_map/ppermute | solution.py:33
  14.2 45.9 %copy-start.8 = (s32[16,8]{0,1:T(8,128)S(1)}, s32[16,8]{0,1:T(8,128)}, u32[]{:S(2)}) copy-start(s32[16,8]{0,1:T(8,128)} %param.9) | copy-start | bytes 1540
  25.0 35.5 %copy-start = (bf16[2064,128]{1,0:T(8,128)(2,1)}, bf16[2064,128]{1,0:T(8,128)(2,1)S(1)}, u32[]{:S(2)}) copy-start(bf16[2064,128]{1,0:T(8,128)(2,1)S(1)} %collective-permute-done.rest_1_) | copy-start | bytes 1585156
  25.0 35.5 %copy-start.2 = (bf16[2064,128]{1,0:T(8,128)(2,1)}, bf16[2064,128]{1,0:T(8,128)(2,1)S(1)}, u32[]{:S(2)}) copy-start(bf16[2064,128]{1,0:T(8,128)(2,1)S(1)} %collective-permute-done.1.rest_2_) | copy-start | bytes 1585156
  28.7 31.4 %all-to-all-start.1 = ((bf16[64,40,128]{2,1,0:T(8,128)(2,1)}), bf16[64,40,128]{2,1,0:T(8,128)(2,1)S(1)}, u32[]{:S(2)}, u32[]{:S(2)}) async-start(bf16[64,40,128]{2,1,0:T(8,128)(2,1)} %fusion.3), calls=%async_computation.1 | async-start | bytes 1310720 | tf_op jit(solution)/shard_map/all_to_all | solution.py:255
  37.0 5.0 %collective-permute-start.5 = (bf16[8,16,16,128]{3,2,1,0:T(8,128)(2,1)S(1)}, bf16[8,16,16,128]{3,2,1,0:T(8,128)(2,1)S(1)}, u32[]{:S(2)}, u32[]{:S(2)}) collective-permute-start(bf16[8,16,16,128]{3,2,1,0:T(8,128)(2,1)S(1)} %all-to-all-done.rest_4_), channel_id=1, source_target_pairs={{0,4},{4,0},{8,12},{12,8},{16,20},{20,16},{24,28},{28,24},{32,36},... | collective-permute-start | bytes 1572872 | tf_op jit(solution)/shard_map/ppermute | solution.py:248
  37.6 21.9 %collective-permute-start.7 = (bf16[8,16,16,128]{3,2,1,0:T(8,128)(2,1)S(1)}, bf16[8,16,16,128]{3,2,1,0:T(8,128)(2,1)}, u32[]{:S(2)}, u32[]{:S(2)}) collective-permute-start(bf16[8,16,16,128]{3,2,1,0:T(8,128)(2,1)S(1)} %all-to-all-done.rest_4_), channel_id=1, source_target_pairs={{0,64},{4,68},{8,72},{12,76},{16,80},{20,84},{24,88},{28,92},{32,9... | collective-permute-start | bytes 1572872 | tf_op jit(solution)/shard_map/ppermute | solution.py:249
  38.9 23.1 %collective-permute-start.9 = (bf16[8,16,16,128]{3,2,1,0:T(8,128)(2,1)S(1)}, bf16[8,16,16,128]{3,2,1,0:T(8,128)(2,1)}, u32[]{:S(2)}, u32[]{:S(2)}) collective-permute-start(bf16[8,16,16,128]{3,2,1,0:T(8,128)(2,1)S(1)} %all-to-all-done.rest_4_), channel_id=1, source_target_pairs={{0,192},{4,196},{8,200},{12,204},{16,208},{20,212},{24,216},{28,22... | collective-permute-start | bytes 1572872 | tf_op jit(solution)/shard_map/ppermute | solution.py:249
  40.4 30.5 %collective-permute-start.11 = (bf16[8,16,16,128]{3,2,1,0:T(8,128)(2,1)S(1)}, bf16[8,16,16,128]{3,2,1,0:T(8,128)(2,1)}, u32[]{:S(2)}, u32[]{:S(2)}) collective-permute-start(bf16[8,16,16,128]{3,2,1,0:T(8,128)(2,1)S(1)} %all-to-all-done.rest_4_), channel_id=1, source_target_pairs={{0,128},{4,132},{8,136},{12,140},{16,144},{20,148},{24,152},{28,15... | collective-permute-start | bytes 1572872 | tf_op jit(solution)/shard_map/ppermute | solution.py:249
  42.0 18.6 %copy-start.4 = (bf16[8,16,16,128]{3,2,1,0:T(8,128)(2,1)}, bf16[8,16,16,128]{3,2,1,0:T(8,128)(2,1)S(1)}, u32[]{:S(2)}) copy-start(bf16[8,16,16,128]{3,2,1,0:T(8,128)(2,1)S(1)} %collective-permute-done.5.rest_5_) | copy-start | bytes 1572868
  42.1 32.5 %collective-permute-start.6 = (bf16[2064,128]{1,0:T(8,128)(2,1)S(1)}, bf16[2064,128]{1,0:T(8,128)(2,1)}, u32[]{:S(2)}, u32[]{:S(2)}) collective-permute-start(bf16[2064,128]{1,0:T(8,128)(2,1)S(1)} %fusion.4.rest_0_), channel_id=1, source_target_pairs={{0,2},{1,3},{2,0},{3,1},{4,6},{5,7},{6,4},{7,5},{8,10},{9,11},{10,... | collective-permute-start | bytes 1585160 | tf_op jit(solution)/shard_map/ppermute | solution.py:33
  59.4 13.9 %collective-permute-start.8 = (bf16[8,16,16,128]{3,2,1,0:T(8,128)(2,1)}, bf16[8,16,16,128]{3,2,1,0:T(8,128)(2,1)}, u32[]{:S(2)}, u32[]{:S(2)}) collective-permute-start(bf16[8,16,16,128]{3,2,1,0:T(8,128)(2,1)} %collective-permute-done.7.rest_6_), channel_id=1, source_target_pairs={{0,4},{4,0},{8,12},{12,8},{16,20},{20,16},{24,28},{28,24},{32,36},... | collective-permute-start | bytes 1572872 | tf_op jit(solution)/shard_map/ppermute | solution.py:271
  60.5 14.4 %copy-start.1 = (bf16[2064,128]{1,0:T(8,128)(2,1)S(1)}, bf16[2064,128]{1,0:T(8,128)(2,1)}, u32[]{:S(2)}) copy-start(bf16[2064,128]{1,0:T(8,128)(2,1)} %copy-done) | copy-start | bytes 1585156
  60.6 14.4 %copy-start.3 = (bf16[2064,128]{1,0:T(8,128)(2,1)S(1)}, bf16[2064,128]{1,0:T(8,128)(2,1)}, u32[]{:S(2)}) copy-start(bf16[2064,128]{1,0:T(8,128)(2,1)} %copy-done.2) | copy-start | bytes 1585156
  60.7 16.4 %copy-start.5 = (bf16[8,16,16,128]{3,2,1,0:T(8,128)(2,1)S(1)}, bf16[8,16,16,128]{3,2,1,0:T(8,128)(2,1)}, u32[]{:S(2)}) copy-start(bf16[8,16,16,128]{3,2,1,0:T(8,128)(2,1)} %copy-done.4) | copy-start | bytes 1572868
  60.7 33.1 %collective-permute-start.2 = (bf16[2064,128]{1,0:T(8,128)(2,1)S(1)}, bf16[2064,128]{1,0:T(8,128)(2,1)S(1)}, u32[]{:S(2)}, u32[]{:S(2)}) collective-permute-start(bf16[2064,128]{1,0:T(8,128)(2,1)S(1)} %fusion.5.s0), channel_id=1, source_target_pairs={{0,1},{1,2},{2,3},{3,0},{4,5},{5,6},{6,7},{7,4},{8,9},{9,10},{10,1... | collective-permute-start | bytes 1585160 | tf_op jit(solution)/shard_map/ppermute | solution.py:33
  62.0 31.9 %collective-permute-start.3 = (bf16[2064,128]{1,0:T(8,128)(2,1)S(1)}, bf16[2064,128]{1,0:T(8,128)(2,1)S(1)}, u32[]{:S(2)}, u32[]{:S(2)}) collective-permute-start(bf16[2064,128]{1,0:T(8,128)(2,1)S(1)} %fusion.5.s0), channel_id=1, source_target_pairs={{0,3},{1,0},{2,1},{3,2},{4,7},{5,4},{6,5},{7,6},{8,11},{9,8},{10,9... | collective-permute-start | bytes 1585160 | tf_op jit(solution)/shard_map/ppermute | solution.py:33
  70.9 23.0 %collective-permute-start.4 = (bf16[2064,128]{1,0:T(8,128)(2,1)S(1)}, bf16[2064,128]{1,0:T(8,128)(2,1)S(1)}, u32[]{:S(2)}, u32[]{:S(2)}) collective-permute-start(bf16[2064,128]{1,0:T(8,128)(2,1)S(1)} %fusion.5.s0), channel_id=1, source_target_pairs={{0,2},{1,3},{2,0},{3,1},{4,6},{5,7},{6,4},{7,5},{8,10},{9,11},{10,... | collective-permute-start | bytes 1585160 | tf_op jit(solution)/shard_map/ppermute | solution.py:33
  73.3 3.0 %collective-permute-start.10 = (bf16[8,16,16,128]{3,2,1,0:T(8,128)(2,1)}, bf16[8,16,16,128]{3,2,1,0:T(8,128)(2,1)S(1)}, u32[]{:S(2)}, u32[]{:S(2)}) collective-permute-start(bf16[8,16,16,128]{3,2,1,0:T(8,128)(2,1)} %collective-permute-done.9.rest_8_), channel_id=1, source_target_pairs={{0,4},{4,0},{8,12},{12,8},{16,20},{20,16},{24,28},{28,24},{32,36},... | collective-permute-start | bytes 1572872 | tf_op jit(solution)/shard_map/ppermute | solution.py:271
  74.6 2.5 %collective-permute-start.12 = (bf16[8,16,16,128]{3,2,1,0:T(8,128)(2,1)}, bf16[8,16,16,128]{3,2,1,0:T(8,128)(2,1)S(1)}, u32[]{:S(2)}, u32[]{:S(2)}) collective-permute-start(bf16[8,16,16,128]{3,2,1,0:T(8,128)(2,1)} %collective-permute-done.11.rest_10_), channel_id=1, source_target_pairs={{0,4},{4,0},{8,12},{12,8},{16,20},{20,16},{24,28},{28,24},{32,36},... | collective-permute-start | bytes 1572872 | tf_op jit(solution)/shard_map/ppermute | solution.py:271
  75.7 18.4 %copy-start.6 = (bf16[256,256]{1,0:T(8,128)(2,1)S(1)}, bf16[256,256]{1,0:T(8,128)(2,1)}, u32[]{:S(2)}) copy-start(bf16[256,256]{1,0:T(8,128)(2,1)} %constant.116.clone.mirror) | copy-start | bytes 393220

commit v4 on v3

--- a/solution.py
+++ b/solution.py
@@ -251,7 +251,7 @@
     messages = jnp.swapaxes(amplitudes.reshape(4, 64, 8, VB), 0, 1).reshape(64, 32, VB)
     tile_ids = jnp.repeat(jnp.swapaxes(amp_ids, 0, 1).reshape(16, 8), 4, axis=0)
     tile_ids = jnp.pad(tile_ids.astype(BF)[:, None, :], ((0, 0), (0, 7), (0, VB - 8)))
-    messages = after(jnp.concatenate([messages, tile_ids], axis=1), along_z, *own_near)
+    messages = after(jnp.concatenate([messages, tile_ids], axis=1), along_z, *own_near, beside)
     received = lax.all_to_all(messages, "pair", 0, 0)
 
     own_shards = [own, *own_near, virt_shift(after(own, beside), 2)]

time: 111 us -> 109 us (0.982); the launches traced: 109 us -> 109 us
    all_to_all x1, waiting for transfers between devices: 3.68 us -> 14.8 us  [body(): along_z = lax.all_to_all(along_z, 'pair', 0, 0, axis_index_groups=groups)]
    ppermute x6, waiting for transfers between devices: 9.97 us -> 0.02 us  [virt_shift(): return lax.ppermute(block, 'virt', [(x, (x + k) % NX) for x in range(NX)])]
    all_to_all x1, starting transfers between devices: 8.3 us -> 6.28 us  [body(): received = lax.all_to_all(messages, 'pair', 0, 0)]
where the time goes in v4:
time: 109 us
  waiting for transfers between devices  38 us (35%)
  starting transfers between devices  33.9 us (31%)
  Pallas kernels  31.6 us (29%)
  local copies, waits for them, and re-layouts  3.65 us (3%)
  other arithmetic  1.14 us (1%)
    ppermute x3, waiting for transfers between devices, body(): lax.ppermute(along_z, 'pair', pair_shift(k, 0, 0))  21.4 us
    pallas_call x1, Pallas kernels, own_ladder(): pl.pallas_call(own_kernel, in_specs=[SMEM] * 2 + [VMEM] * 12, out_specs=[...  16.8 us
    pallas_call x1, Pallas kernels, add_turned(): pl.pallas_call(turn_kernel, in_specs=[VMEM] * 6 + [ANY] * 2, out_specs=AN...  14.8 us
    all_to_all x1, waiting for transfers between devices, body(): along_z = lax.all_to_all(along_z, 'pair', 0, 0, axis_index_groups=groups)  14.8 us
    ppermute x6, starting transfers between devices, virt_shift(): return lax.ppermute(block, 'virt', [(x, (x + k) % NX) for x in range(NX)])  10.4 us
    all_to_all x1, starting transfers between devices, body(): along_z = lax.all_to_all(along_z, 'pair', 0, 0, axis_index_groups=groups)  9.01 us
    all_to_all x1, starting transfers between devices, body(): received = lax.all_to_all(messages, 'pair', 0, 0)  6.28 us
    ppermute x3, starting transfers between devices, body(): lax.ppermute(along_z, 'pair', pair_shift(k, 0, 0))  4.61 us
  transfers between devices with their start and end apart: 15, of which 6 were waited for; matrix products, arithmetic and copies ran while one was open for 3% of the time, Pallas kernels for 15%

profile of v4, /device:TPU:1, one launch (start us, length us, event | category | flops | bytes accessed | tf_op | source)
XLA Modules:
  0.0 108.7 jit_solution(303357542173607284)
XLA Ops:
  0.0 1.8 %broadcast_in_dim.13 = bf16[8,16,16,128]{3,2,1,0:T(8,128)(2,1)} broadcast(bf16[16,16,128]{2,1,0:T(8,128)(2,1)} %param.8), dimensions={1,2,3} | broadcast | bytes 589824 | tf_op jit(solution)/shard_map/broadcast_in_dim | solution.py:246
  1.8 9.0 %all-to-all-start = ((bf16[8,16,16,128]{3,2,1,0:T(8,128)(2,1)}), bf16[8,16,16,128]{3,2,1,0:T(8,128)(2,1)S(1)}, u32[]{:S(2)}, u32[]{:S(2)}) async-start(bf16[8,16,16,128]{3,2,1,0:T(8,128)(2,1)} %broadcast_in_dim.13), calls=%async_computation | async-start | bytes 1048576 | tf_op jit(solution)/shard_map/all_to_all | solution.py:247
  10.8 0.1 copy.33
  10.9 0.1 reshape.196
  11.2 1.3 %collective-permute-start = (bf16[2064,128]{1,0:T(8,128)(2,1)S(1)}, bf16[2064,128]{1,0:T(8,128)(2,1)S(1)}, u32[]{:S(2)}, u32[]{:S(2)}) collective-permute-start(bf16[2064,128]{1,0:T(8,128)(2,1)S(1)} %fusion.4.rest_0_), channel_id=1, source_target_pairs={{0,1},{1,2},{2,3},{3,0},{4,5},{5,6},{6,7},{7,4},{8,9},{9,10},{10,1... | collective-permute-start | bytes 1585160 | tf_op jit(solution)/shard_map/ppermute | solution.py:33
  12.5 1.5 %collective-permute-start.1 = (bf16[2064,128]{1,0:T(8,128)(2,1)S(1)}, bf16[2064,128]{1,0:T(8,128)(2,1)S(1)}, u32[]{:S(2)}, u32[]{:S(2)}) collective-permute-start(bf16[2064,128]{1,0:T(8,128)(2,1)S(1)} %fusion.4.rest_0_), channel_id=1, source_target_pairs={{0,3},{1,0},{2,1},{3,2},{4,7},{5,4},{6,5},{7,6},{8,11},{9,8},{10,9... | collective-permute-start | bytes 1585160 | tf_op jit(solution)/shard_map/ppermute | solution.py:33
  13.9 14.8 %all-to-all-done.rest_4_ = bf16[8,16,16,128]{3,2,1,0:T(8,128)(2,1)S(1)} async-done(((bf16[8,16,16,128]{3,2,1,0:T(8,128)(2,1)}), bf16[8,16,16,128]{3,2,1,0:T(8,128)(2,1)S(1)}, u32[]{:S(2)}, u32[]{:S(2)}) %all-to-all-start) | async-done | bytes 524320 | tf_op jit(solution)/shard_map/all_to_all | solution.py:247
  28.7 0.5 collective-permute-start.2
  29.4 0.1 copy.39
  29.5 0.9 fusion.3
  30.4 0.4 collective-permute-done.2.rest_5_
  30.8 6.3 %all-to-all-start.1 = ((bf16[64,40,128]{2,1,0:T(8,128)(2,1)}), bf16[64,40,128]{2,1,0:T(8,128)(2,1)S(1)}, u32[]{:S(2)}, u32[]{:S(2)}) async-start(bf16[64,40,128]{2,1,0:T(8,128)(2,1)} %fusion.3), calls=%async_computation.1 | async-start | bytes 1310720 | tf_op jit(solution)/shard_map/all_to_all | solution.py:255
  37.1 1.5 %collective-permute-start.7 = (bf16[8,16,16,128]{3,2,1,0:T(8,128)(2,1)S(1)}, bf16[8,16,16,128]{3,2,1,0:T(8,128)(2,1)}, u32[]{:S(2)}, u32[]{:S(2)}) collective-permute-start(bf16[8,16,16,128]{3,2,1,0:T(8,128)(2,1)S(1)} %all-to-all-done.rest_4_), channel_id=1, source_target_pairs={{0,64},{4,68},{8,72},{12,76},{16,80},{20,84},{24,88},{28,92},{32,9... | collective-permute-start | bytes 1572872 | tf_op jit(solution)/shard_map/ppermute | solution.py:249
  38.5 1.5 %collective-permute-start.9 = (bf16[8,16,16,128]{3,2,1,0:T(8,128)(2,1)S(1)}, bf16[8,16,16,128]{3,2,1,0:T(8,128)(2,1)}, u32[]{:S(2)}, u32[]{:S(2)}) collective-permute-start(bf16[8,16,16,128]{3,2,1,0:T(8,128)(2,1)S(1)} %all-to-all-done.rest_4_), channel_id=1, source_target_pairs={{0,192},{4,196},{8,200},{12,204},{16,208},{20,212},{24,216},{28,22... | collective-permute-start | bytes 1572872 | tf_op jit(solution)/shard_map/ppermute | solution.py:249
  40.1 1.6 %collective-permute-start.11 = (bf16[8,16,16,128]{3,2,1,0:T(8,128)(2,1)S(1)}, bf16[8,16,16,128]{3,2,1,0:T(8,128)(2,1)}, u32[]{:S(2)}, u32[]{:S(2)}) collective-permute-start(bf16[8,16,16,128]{3,2,1,0:T(8,128)(2,1)S(1)} %all-to-all-done.rest_4_), channel_id=1, source_target_pairs={{0,128},{4,132},{8,136},{12,140},{16,144},{20,148},{24,152},{28,15... | collective-permute-start | bytes 1572872 | tf_op jit(solution)/shard_map/ppermute | solution.py:249
  41.7 2.4 %collective-permute-start.6 = (bf16[2064,128]{1,0:T(8,128)(2,1)S(1)}, bf16[2064,128]{1,0:T(8,128)(2,1)}, u32[]{:S(2)}, u32[]{:S(2)}) collective-permute-start(bf16[2064,128]{1,0:T(8,128)(2,1)S(1)} %fusion.4.rest_0_), channel_id=1, source_target_pairs={{0,2},{1,3},{2,0},{3,1},{4,6},{5,7},{6,4},{7,5},{8,10},{9,11},{10,... | collective-permute-start | bytes 1585160 | tf_op jit(solution)/shard_map/ppermute | solution.py:33
  44.1 14.9 %collective-permute-done.7.rest_6_ = bf16[8,16,16,128]{3,2,1,0:T(8,128)(2,1)} collective-permute-done((bf16[8,16,16,128]{3,2,1,0:T(8,128)(2,1)S(1)}, bf16[8,16,16,128]{3,2,1,0:T(8,128)(2,1)}, u32[]{:S(2)}, u32[]{:S(2)}) %collective-permute-start.7) | collective-permute-done | bytes 524320 | tf_op jit(solution)/shard_map/ppermute | solution.py:249
  59.1 1.3 %collective-permute-start.8 = (bf16[8,16,16,128]{3,2,1,0:T(8,128)(2,1)}, bf16[8,16,16,128]{3,2,1,0:T(8,128)(2,1)}, u32[]{:S(2)}, u32[]{:S(2)}) collective-permute-start(bf16[8,16,16,128]{3,2,1,0:T(8,128)(2,1)} %collective-permute-done.7.rest_6_), channel_id=1, source_target_pairs={{0,4},{4,0},{8,12},{12,8},{16,20},{20,16},{24,28},{28,24},{32,36},... | collective-permute-start | bytes 1572872 | tf_op jit(solution)/shard_map/ppermute | solution.py:271
  60.4 0.1 slice_reduce_fusion
  61.0 1.3 %collective-permute-start.3 = (bf16[2064,128]{1,0:T(8,128)(2,1)S(1)}, bf16[2064,128]{1,0:T(8,128)(2,1)S(1)}, u32[]{:S(2)}, u32[]{:S(2)}) collective-permute-start(bf16[2064,128]{1,0:T(8,128)(2,1)S(1)} %fusion.5.s0), channel_id=1, source_target_pairs={{0,1},{1,2},{2,3},{3,0},{4,5},{5,6},{6,7},{7,4},{8,9},{9,10},{10,1... | collective-permute-start | bytes 1585160 | tf_op jit(solution)/shard_map/ppermute | solution.py:33
  62.2 1.6 %collective-permute-start.4 = (bf16[2064,128]{1,0:T(8,128)(2,1)S(1)}, bf16[2064,128]{1,0:T(8,128)(2,1)S(1)}, u32[]{:S(2)}, u32[]{:S(2)}) collective-permute-start(bf16[2064,128]{1,0:T(8,128)(2,1)S(1)} %fusion.5.s0), channel_id=1, source_target_pairs={{0,3},{1,0},{2,1},{3,2},{4,7},{5,4},{6,5},{7,6},{8,11},{9,8},{10,9... | collective-permute-start | bytes 1585160 | tf_op jit(solution)/shard_map/ppermute | solution.py:33
  63.8 6.5 %collective-permute-done.11.rest_10_ = bf16[8,16,16,128]{3,2,1,0:T(8,128)(2,1)} collective-permute-done((bf16[8,16,16,128]{3,2,1,0:T(8,128)(2,1)S(1)}, bf16[8,16,16,128]{3,2,1,0:T(8,128)(2,1)}, u32[]{:S(2)}, u32[]{:S(2)}) %collective-permute-start.11) | collective-permute-done | bytes 524320 | tf_op jit(solution)/shard_map/ppermute | solution.py:249
  70.3 2.4 %collective-permute-start.5 = (bf16[2064,128]{1,0:T(8,128)(2,1)S(1)}, bf16[2064,128]{1,0:T(8,128)(2,1)S(1)}, u32[]{:S(2)}, u32[]{:S(2)}) collective-permute-start(bf16[2064,128]{1,0:T(8,128)(2,1)S(1)} %fusion.5.s0), channel_id=1, source_target_pairs={{0,2},{1,3},{2,0},{3,1},{4,6},{5,7},{6,4},{7,5},{8,10},{9,11},{10,... | collective-permute-start | bytes 1585160 | tf_op jit(solution)/shard_map/ppermute | solution.py:33
  72.7 1.5 %collective-permute-start.10 = (bf16[8,16,16,128]{3,2,1,0:T(8,128)(2,1)}, bf16[8,16,16,128]{3,2,1,0:T(8,128)(2,1)S(1)}, u32[]{:S(2)}, u32[]{:S(2)}) collective-permute-start(bf16[8,16,16,128]{3,2,1,0:T(8,128)(2,1)} %collective-permute-done.9.rest_8_), channel_id=1, source_target_pairs={{0,4},{4,0},{8,12},{12,8},{16,20},{20,16},{24,28},{28,24},{32,36},... | collective-permute-start | bytes 1572872 | tf_op jit(solution)/shard_map/ppermute | solution.py:271
  74.2 0.3 collective-permute-start.12
  74.5 0.1 multiply_reduce_fusion
  74.6 0.7 slice.46
  75.3 0.6 collective-permute-done.10.rest_9_
  75.9 0.7 collective-permute-done.12.rest_11_
  76.7 16.8 %own_ladder.1 = (bf16[1024,2048]{1,0:T(8,128)(2,1)}, bf16[2048,2048]{1,0:T(8,128)(2,1)}) custom-call(s32[16,64]{1,0:T(8,128)S(1)} %multiply_add_fusion.rows, s32[4,128]{1,0:T(4,128)S(1)} %maximum_convert_fusion.1.amp_ids, bf16[2064,128]{1,0:T(8,128)(2,1)S(1)} %fusion.4.rest_0_, bf16[2064,128]{1,0:T(8,128)(2,1)S(1)} %copy-done.1, ...), custom_call_target="tpu_custom_call" | custom-call | tf_op jit(solution)/shard_map/own_ladder/pallas_call | solution.py:136
  93.6 0.1 copy.36
  93.7 14.8 %add_turned.1 = bf16[1024,2048]{1,0:T(8,128)(2,1)} custom-call(f32[256,8]{1,0:T(8,128)S(1)} %bitcast.25, bf16[2064,128]{1,0:T(8,128)(2,1)S(1)} %fusion.5.s0, bf16[2064,128]{1,0:T(8,128)(2,1)S(1)} %collective-permute-done.3.s1, bf16[2064,128]{1,0:T(8,128)(2,1)S(1)} %collective-permute-done.4.s2, bf16[2064,128]{1,0:T(8,128)(2,1)S(1)} %collective-permute-done.5.s3, ...), custom_call_target="tpu_custom_call" | custom-call | tf_op jit(solution)/shard_map/add_turned/pallas_call | solution.py:217
  (54 shorter events, 0.8 us)
Async XLA Ops:
  0.0 10.8 %copy-start.9 = (s32[4,16,2]{1,2,0:T(2,128)S(1)}, s32[4,16,2]{1,2,0:T(2,128)}, u32[]{:S(2)}) copy-start(s32[4,16,2]{1,2,0:T(2,128)} %param.7) | copy-start | bytes 1540
  0.0 11.1 %copy-start.7 = (bf16[4,256,2,128]{3,2,1,0:T(2,128)(2,1)S(1)}, bf16[4,256,2,128]{3,2,1,0:T(2,128)(2,1)}, u32[]{:S(2)}) copy-start(bf16[4,256,2,128]{3,2,1,0:T(2,128)(2,1)} %param.6) | copy-start | bytes 1572868
  1.8 27.0 %all-to-all-start = ((bf16[8,16,16,128]{3,2,1,0:T(8,128)(2,1)}), bf16[8,16,16,128]{3,2,1,0:T(8,128)(2,1)S(1)}, u32[]{:S(2)}, u32[]{:S(2)}) async-start(bf16[8,16,16,128]{3,2,1,0:T(8,128)(2,1)} %broadcast_in_dim.13), calls=%async_computation | async-start | bytes 1048576 | tf_op jit(solution)/shard_map/all_to_all | solution.py:247
  11.2 19.2 %collective-permute-start = (bf16[2064,128]{1,0:T(8,128)(2,1)S(1)}, bf16[2064,128]{1,0:T(8,128)(2,1)S(1)}, u32[]{:S(2)}, u32[]{:S(2)}) collective-permute-start(bf16[2064,128]{1,0:T(8,128)(2,1)S(1)} %fusion.4.rest_0_), channel_id=1, source_target_pairs={{0,1},{1,2},{2,3},{3,0},{4,5},{5,6},{6,7},{7,4},{8,9},{9,10},{10,1... | collective-permute-start | bytes 1585160 | tf_op jit(solution)/shard_map/ppermute | solution.py:33
  12.5 17.9 %collective-permute-start.1 = (bf16[2064,128]{1,0:T(8,128)(2,1)S(1)}, bf16[2064,128]{1,0:T(8,128)(2,1)S(1)}, u32[]{:S(2)}, u32[]{:S(2)}) collective-permute-start(bf16[2064,128]{1,0:T(8,128)(2,1)S(1)} %fusion.4.rest_0_), channel_id=1, source_target_pairs={{0,3},{1,0},{2,1},{3,2},{4,7},{5,4},{6,5},{7,6},{8,11},{9,8},{10,9... | collective-permute-start | bytes 1585160 | tf_op jit(solution)/shard_map/ppermute | solution.py:33
  28.7 2.0 %collective-permute-start.2 = (bf16[8,16,16,128]{3,2,1,0:T(8,128)(2,1)S(1)}, bf16[8,16,16,128]{3,2,1,0:T(8,128)(2,1)S(1)}, u32[]{:S(2)}, u32[]{:S(2)}) collective-permute-start(bf16[8,16,16,128]{3,2,1,0:T(8,128)(2,1)S(1)} %all-to-all-done.rest_4_), channel_id=1, source_target_pairs={{0,4},{4,0},{8,12},{12,8},{16,20},{20,16},{24,28},{28,24},{32,36},... | collective-permute-start | bytes 1572872 | tf_op jit(solution)/shard_map/ppermute | solution.py:248
  29.5 30.9 %copy-start.8 = (s32[16,8]{0,1:T(8,128)S(1)}, s32[16,8]{0,1:T(8,128)}, u32[]{:S(2)}) copy-start(s32[16,8]{0,1:T(8,128)} %param.9) | copy-start | bytes 1540
  30.4 30.4 %copy-start = (bf16[2064,128]{1,0:T(8,128)(2,1)}, bf16[2064,128]{1,0:T(8,128)(2,1)S(1)}, u32[]{:S(2)}) copy-start(bf16[2064,128]{1,0:T(8,128)(2,1)S(1)} %collective-permute-done.rest_1_) | copy-start | bytes 1585156
  30.4 30.4 %copy-start.2 = (bf16[2064,128]{1,0:T(8,128)(2,1)}, bf16[2064,128]{1,0:T(8,128)(2,1)S(1)}, u32[]{:S(2)}) copy-start(bf16[2064,128]{1,0:T(8,128)(2,1)S(1)} %collective-permute-done.1.rest_2_) | copy-start | bytes 1585156
  30.8 30.0 %copy-start.4 = (bf16[8,16,16,128]{3,2,1,0:T(8,128)(2,1)}, bf16[8,16,16,128]{3,2,1,0:T(8,128)(2,1)S(1)}, u32[]{:S(2)}) copy-start(bf16[8,16,16,128]{3,2,1,0:T(8,128)(2,1)S(1)} %collective-permute-done.2.rest_5_) | copy-start | bytes 1572868
  30.8 29.6 %all-to-all-start.1 = ((bf16[64,40,128]{2,1,0:T(8,128)(2,1)}), bf16[64,40,128]{2,1,0:T(8,128)(2,1)S(1)}, u32[]{:S(2)}, u32[]{:S(2)}) async-start(bf16[64,40,128]{2,1,0:T(8,128)(2,1)} %fusion.3), calls=%async_computation.1 | async-start | bytes 1310720 | tf_op jit(solution)/shard_map/all_to_all | solution.py:255
  37.1 22.0 %collective-permute-start.7 = (bf16[8,16,16,128]{3,2,1,0:T(8,128)(2,1)S(1)}, bf16[8,16,16,128]{3,2,1,0:T(8,128)(2,1)}, u32[]{:S(2)}, u32[]{:S(2)}) collective-permute-start(bf16[8,16,16,128]{3,2,1,0:T(8,128)(2,1)S(1)} %all-to-all-done.rest_4_), channel_id=1, source_target_pairs={{0,64},{4,68},{8,72},{12,76},{16,80},{20,84},{24,88},{28,92},{32,9... | collective-permute-start | bytes 1572872 | tf_op jit(solution)/shard_map/ppermute | solution.py:249
  38.5 23.7 %collective-permute-start.9 = (bf16[8,16,16,128]{3,2,1,0:T(8,128)(2,1)S(1)}, bf16[8,16,16,128]{3,2,1,0:T(8,128)(2,1)}, u32[]{:S(2)}, u32[]{:S(2)}) collective-permute-start(bf16[8,16,16,128]{3,2,1,0:T(8,128)(2,1)S(1)} %all-to-all-done.rest_4_), channel_id=1, source_target_pairs={{0,192},{4,196},{8,200},{12,204},{16,208},{20,212},{24,216},{28,22... | collective-permute-start | bytes 1572872 | tf_op jit(solution)/shard_map/ppermute | solution.py:249
  40.1 30.2 %collective-permute-start.11 = (bf16[8,16,16,128]{3,2,1,0:T(8,128)(2,1)S(1)}, bf16[8,16,16,128]{3,2,1,0:T(8,128)(2,1)}, u32[]{:S(2)}, u32[]{:S(2)}) collective-permute-start(bf16[8,16,16,128]{3,2,1,0:T(8,128)(2,1)S(1)} %all-to-all-done.rest_4_), channel_id=1, source_target_pairs={{0,128},{4,132},{8,136},{12,140},{16,144},{20,148},{24,152},{28,15... | collective-permute-start | bytes 1572872 | tf_op jit(solution)/shard_map/ppermute | solution.py:249
  41.7 32.5 %collective-permute-start.6 = (bf16[2064,128]{1,0:T(8,128)(2,1)S(1)}, bf16[2064,128]{1,0:T(8,128)(2,1)}, u32[]{:S(2)}, u32[]{:S(2)}) collective-permute-start(bf16[2064,128]{1,0:T(8,128)(2,1)S(1)} %fusion.4.rest_0_), channel_id=1, source_target_pairs={{0,2},{1,3},{2,0},{3,1},{4,6},{5,7},{6,4},{7,5},{8,10},{9,11},{10,... | collective-permute-start | bytes 1585160 | tf_op jit(solution)/shard_map/ppermute | solution.py:33
  59.1 13.7 %collective-permute-start.8 = (bf16[8,16,16,128]{3,2,1,0:T(8,128)(2,1)}, bf16[8,16,16,128]{3,2,1,0:T(8,128)(2,1)}, u32[]{:S(2)}, u32[]{:S(2)}) collective-permute-start(bf16[8,16,16,128]{3,2,1,0:T(8,128)(2,1)} %collective-permute-done.7.rest_6_), channel_id=1, source_target_pairs={{0,4},{4,0},{8,12},{12,8},{16,20},{20,16},{24,28},{28,24},{32,36},... | collective-permute-start | bytes 1572872 | tf_op jit(solution)/shard_map/ppermute | solution.py:271
  60.8 13.8 %copy-start.1 = (bf16[2064,128]{1,0:T(8,128)(2,1)S(1)}, bf16[2064,128]{1,0:T(8,128)(2,1)}, u32[]{:S(2)}) copy-start(bf16[2064,128]{1,0:T(8,128)(2,1)} %copy-done) | copy-start | bytes 1585156
  60.8 13.8 %copy-start.3 = (bf16[2064,128]{1,0:T(8,128)(2,1)S(1)}, bf16[2064,128]{1,0:T(8,128)(2,1)}, u32[]{:S(2)}) copy-start(bf16[2064,128]{1,0:T(8,128)(2,1)} %copy-done.2) | copy-start | bytes 1585156
  60.8 15.9 %copy-start.5 = (bf16[8,16,16,128]{3,2,1,0:T(8,128)(2,1)S(1)}, bf16[8,16,16,128]{3,2,1,0:T(8,128)(2,1)}, u32[]{:S(2)}) copy-start(bf16[8,16,16,128]{3,2,1,0:T(8,128)(2,1)} %copy-done.4) | copy-start | bytes 1572868
  61.0 32.5 %collective-permute-start.3 = (bf16[2064,128]{1,0:T(8,128)(2,1)S(1)}, bf16[2064,128]{1,0:T(8,128)(2,1)S(1)}, u32[]{:S(2)}, u32[]{:S(2)}) collective-permute-start(bf16[2064,128]{1,0:T(8,128)(2,1)S(1)} %fusion.5.s0), channel_id=1, source_target_pairs={{0,1},{1,2},{2,3},{3,0},{4,5},{5,6},{6,7},{7,4},{8,9},{9,10},{10,1... | collective-permute-start | bytes 1585160 | tf_op jit(solution)/shard_map/ppermute | solution.py:33
  62.2 31.3 %collective-permute-start.4 = (bf16[2064,128]{1,0:T(8,128)(2,1)S(1)}, bf16[2064,128]{1,0:T(8,128)(2,1)S(1)}, u32[]{:S(2)}, u32[]{:S(2)}) collective-permute-start(bf16[2064,128]{1,0:T(8,128)(2,1)S(1)} %fusion.5.s0), channel_id=1, source_target_pairs={{0,3},{1,0},{2,1},{3,2},{4,7},{5,4},{6,5},{7,6},{8,11},{9,8},{10,9... | collective-permute-start | bytes 1585160 | tf_op jit(solution)/shard_map/ppermute | solution.py:33
  70.3 23.2 %collective-permute-start.5 = (bf16[2064,128]{1,0:T(8,128)(2,1)S(1)}, bf16[2064,128]{1,0:T(8,128)(2,1)S(1)}, u32[]{:S(2)}, u32[]{:S(2)}) collective-permute-start(bf16[2064,128]{1,0:T(8,128)(2,1)S(1)} %fusion.5.s0), channel_id=1, source_target_pairs={{0,2},{1,3},{2,0},{3,1},{4,6},{5,7},{6,4},{7,5},{8,10},{9,11},{10,... | collective-permute-start | bytes 1585160 | tf_op jit(solution)/shard_map/ppermute | solution.py:33
  72.7 3.2 %collective-permute-start.10 = (bf16[8,16,16,128]{3,2,1,0:T(8,128)(2,1)}, bf16[8,16,16,128]{3,2,1,0:T(8,128)(2,1)S(1)}, u32[]{:S(2)}, u32[]{:S(2)}) collective-permute-start(bf16[8,16,16,128]{3,2,1,0:T(8,128)(2,1)} %collective-permute-done.9.rest_8_), channel_id=1, source_target_pairs={{0,4},{4,0},{8,12},{12,8},{16,20},{20,16},{24,28},{28,24},{32,36},... | collective-permute-start | bytes 1572872 | tf_op jit(solution)/shard_map/ppermute | solution.py:271
  74.2 2.5 %collective-permute-start.12 = (bf16[8,16,16,128]{3,2,1,0:T(8,128)(2,1)}, bf16[8,16,16,128]{3,2,1,0:T(8,128)(2,1)S(1)}, u32[]{:S(2)}, u32[]{:S(2)}) collective-permute-start(bf16[8,16,16,128]{3,2,1,0:T(8,128)(2,1)} %collective-permute-done.11.rest_10_), channel_id=1, source_target_pairs={{0,4},{4,0},{8,12},{12,8},{16,20},{20,16},{24,28},{28,24},{32,36},... | collective-permute-start | bytes 1572872 | tf_op jit(solution)/shard_map/ppermute | solution.py:271
  75.3 18.4 %copy-start.6 = (bf16[256,256]{1,0:T(8,128)(2,1)S(1)}, bf16[256,256]{1,0:T(8,128)(2,1)}, u32[]{:S(2)}) copy-start(bf16[256,256]{1,0:T(8,128)(2,1)} %constant.116.clone.mirror) | copy-start | bytes 393220
